TPU v7x, 512 devices: a whole 4x4x16 slice. The times are simulated.
512 devices in a mesh: slab: 32 (over x, y, core), grp: 16 (over z).
Axes of the slice: x: 4, y: 4, z: 16, core: 2. Of those that a mesh axis runs over, the one named last changes fastest.
Arguments:
- fields: bfloat16 [27, 1048576], P(None, ('slab', 'grp')), may hold values from -5 to 5
- spline: bfloat16 [3, 8, 4, 2097152], P(None, None, None, ('slab', 'grp')), may hold values from -4 to 4
- measured: float32 [3, 2097152], P(None, ('slab', 'grp')), may hold values from -6 to 6
- confidence: float32 [2097152], P(('slab', 'grp')), may hold values from 0.05 to 3
- block_ids: int32 [32768, 4], P(('slab', 'grp')), may hold values from 0 to 63, all different within a row
- live: int32 [32768], P(('slab', 'grp')), may hold values from 1 to 4
- owners: int32 [2097152, 1], P(('slab', 'grp')), may hold values from 0 to 511; in each aligned block of 4096 rows (0 to 4095, 4096 to 8191, ...) at most 16 rows name the same one
Outputs:
- received: float32 [8, 4194304], P(None, ('slab', 'grp'))
- update: float32 [8], replicated
Inputs may be any that keep to these rules, and one draw needn't show every extreme that they name: `block_ids`: each row names 4 different voxel blocks of its own slab. `owners`: among the 4096 subsets of one device, at most 16 have the same owner, and some owner gets exactly 16 of them.
All inputs are finite; a program needn't handle non-finite values.
Results may differ from a plain program's by a relative error of at most 0.0018.
Values may be sent and summed in bfloat16 or wider, within the bound.
A program may use at most 128 MiB of HBM per device.

v0:
```python
import jax
import jax.numpy as jnp
from jax import lax
from jax.sharding import PartitionSpec as P

damping = 0.05


def build_tiles(spline_part, live_part):
    along_z = spline_part[0].astype(jnp.float32)
    along_y = spline_part[1].astype(jnp.float32)
    along_x = spline_part[2].astype(jnp.float32)
    edge_cells = along_z.shape[0]
    product = along_z[:, None, None] * along_y[None, :, None]
    product = product * along_x[None, None, :]
    product = product.reshape((edge_cells * edge_cells * edge_cells,) + along_z.shape[1:])
    slot_iota = lax.broadcasted_iota(jnp.int32, (along_z.shape[1], along_z.shape[2]), 0)
    keep_mask = (slot_iota < live_part[None, :]).astype(jnp.float32)
    return (product * keep_mask[None, :, :, None]).astype(jnp.bfloat16)


def local_normal(modelled, measured_rows, confidence_row, parameters):
    residual = measured_rows - modelled[0:3]
    flat_sens = modelled[3:].reshape(parameters, -1)
    weighted = jnp.broadcast_to(confidence_row[None, :], residual.shape).reshape(-1)
    hessian = jnp.einsum(
        "ai,bi->ab", flat_sens, flat_sens * weighted[None, :], precision=lax.Precision.HIGHEST
    )
    gradient = jnp.dot(flat_sens, residual.reshape(-1) * weighted, precision=lax.Precision.HIGHEST)
    return (residual, hessian, gradient)


def solve_normal(hessian, gradient):
    damped = hessian + damping * jnp.diag(jnp.diag(hessian))
    factor = jnp.linalg.cholesky(damped)
    length = gradient.shape[0]
    forward = []
    for row_index in range(length):
        running = gradient[row_index]
        for col_index in range(row_index):
            running = running - factor[row_index, col_index] * forward[col_index]
        forward.append(running / factor[row_index, row_index])
    backward = [None] * length
    for row_index in reversed(range(length)):
        running = forward[row_index]
        for col_index in range(row_index + 1, length):
            running = running - factor[col_index, row_index] * backward[col_index]
        backward[row_index] = running / factor[row_index, row_index]
    return jnp.stack(backward)


def assemble(modelled_rows, residual, confidence_row, update):
    parameters = update.shape[0]
    sensitivity = modelled_rows[3:].reshape(parameters, 3, -1)
    predicted = jnp.einsum("acs,a->cs", sensitivity, update, precision=lax.Precision.HIGHEST)
    remaining = residual - predicted
    return jnp.concatenate(
        [
            modelled_rows[0:3] + predicted,
            confidence_row[None, :] * remaining,
            confidence_row[None, :],
            confidence_row[None, :] * jnp.sum(remaining * remaining, axis=0, keepdims=True),
        ],
        axis=0,
    )


def place_slots(payload, destination, peer_count, capacity):
    subset_count = destination.shape[0]
    permutation = jnp.argsort(destination, stable=True)
    ordered = destination[permutation]
    run_start = jnp.searchsorted(ordered, ordered, side="left")
    rank_sorted = jnp.arange(subset_count, dtype=jnp.int32) - run_start
    rank_within = jnp.zeros((subset_count,), jnp.int32).at[permutation].set(rank_sorted)
    column = destination * capacity + rank_within
    return (
        jnp.zeros((payload.shape[0], peer_count * capacity), payload.dtype)
        .at[:, column]
        .set(payload)
    )


def block_group(total_blocks):
    chosen = 1
    for candidate in range(1, 17):
        if total_blocks % candidate == 0:
            chosen = candidate
    return chosen


def body(fields, spline, measured, confidence, block_ids, live, owners):
    channels = fields.shape[0]
    sb_count = block_ids.shape[0]
    subset_count = confidence.shape[0]
    subs_block = subset_count // sb_count
    edge_cells = spline.shape[1]
    tile_slots = spline.shape[2]
    block_cells = edge_cells * edge_cells * edge_cells
    parameters = (channels - 3) // 3
    slab_count = lax.axis_size("slab")
    grp_count = lax.axis_size("grp")
    peer_count = slab_count * grp_count
    capacity = 2 * subset_count // peer_count
    slab_fields = lax.all_gather(fields, "grp", axis=1, tiled=True)
    pool_blocks = slab_fields.reshape(channels, -1, block_cells)
    group_size = block_group(sb_count)
    spline_view = spline.reshape(3, edge_cells, tile_slots, sb_count, subs_block)

    def interp_step(turn_index, modelled):
        offset_blocks = turn_index * group_size
        id_part = lax.dynamic_slice_in_dim(block_ids, offset_blocks, group_size, 0)
        live_part = lax.dynamic_slice_in_dim(live, offset_blocks, group_size, 0)
        spline_part = lax.dynamic_slice_in_dim(spline_view, offset_blocks, group_size, 3)
        picked = jnp.take(pool_blocks, id_part, axis=1)
        tile_set = build_tiles(spline_part, live_part)
        block_part = jnp.einsum(
            "cnkv,vkns->cns", picked, tile_set, preferred_element_type=jnp.float32
        )
        return lax.dynamic_update_slice_in_dim(modelled, block_part, offset_blocks, 1)

    modelled = lax.fori_loop(
        0,
        sb_count // group_size,
        interp_step,
        jnp.zeros((channels, sb_count, subs_block), jnp.float32),
    )
    modelled = modelled.reshape(channels, subset_count)
    residual, hess_local, grad_local = local_normal(modelled, measured, confidence, parameters)
    destination = owners[:, 0]
    hessian, gradient = lax.psum((hess_local, grad_local), ("slab", "grp"))
    update = solve_normal(hessian, gradient)
    payload = assemble(modelled, residual, confidence, update)
    placed = place_slots(payload, destination, peer_count, capacity).reshape(
        8, slab_count, grp_count, capacity
    )
    arrived = lax.all_to_all(
        lax.all_to_all(placed, "slab", split_axis=1, concat_axis=1, tiled=True),
        "grp",
        split_axis=2,
        concat_axis=2,
        tiled=True,
    )
    received = arrived.reshape(8, peer_count * capacity)
    return (received, update)


def solution(mesh):
    placed = (
        P(None, ("slab", "grp")),
        P(None, None, None, ("slab", "grp")),
        P(None, ("slab", "grp")),
        P(("slab", "grp")),
        P(("slab", "grp"), None),
        P(("slab", "grp")),
        P(("slab", "grp"), None),
    )
    return jax.shard_map(
        body, mesh=mesh, in_specs=placed, out_specs=(P(None, ("slab", "grp")), P()), check_vma=False
    )
```

profile of v0, /device:TPU:1, one launch (start us, length us, event | category | flops | bytes accessed | tf_op | source)
XLA Modules:
  0.0 780.4 jit_solution(2559715062802014946)
XLA Ops:
  7.2 0.7 all-gather.2.cloned.1.call-update
  7.9 6.5 sort.17
  14.4 23.0 %gather_fusion.2 = s32[4096]{0:T(1024)S(1)} fusion(s32[4096]{0:T(1024)S(1)} %bitcast.139, s32[4096]{0:T(1024)S(1)} %get-tuple-element.255), kind=kCustom, calls=%fused_computation.2 | custom fusion | bytes 49152 | tf_op jit(solution)/shard_map/gather | solution.py:71
  37.5 300.6 %while.39 = (s32[]{:T(128)}, u32[4096]{0:T(1024)S(1)}, u32[4096]{0:T(1024)S(1)}, s32[4096]{0:T(1024)S(1)}, s32[]{:T(128)}, /*index=5*/s32[]{:T(128)}, s32[]{}) while((s32[]{:T(128)}, u32[4096]{0:T(1024)S(1)}, u32[4096]{0:T(1024)S(1)}, s32[4096]{0:T(1024)S(1)}, s32[]{:T(128)}, /*index=5*/s32[]{:T(128)}, s32[]{}) %tuple.117), condition=%wide.region_2.3_spmd.clone, body=%wide.region_1.0_spmd.clone.sunk | while | flops 77828 | bytes 270437 | solution.py:72
  37.5 23.0 %gather_fusion.1 = s32[4096]{0:T(1024)S(1)} fusion(s32[4096]{0:T(1024)S(1)} %get-tuple-element.390, u32[4096]{0:T(1024)S(1)} %broadcast_clamp_fusion.3), kind=kCustom, calls=%fused_computation.clone.clone.1 | custom fusion | bytes 49152 | tf_op jit(solution)/shard_map/jit(searchsorted)/jit(_searchsorted_scan_impl)/vmap(jit(_searchsorted_scan_impl))/while/body/eval_jaxpr/gather | solution.py:72
  60.7 23.0 %gather_fusion.1 = s32[4096]{0:T(1024)S(1)} fusion(s32[4096]{0:T(1024)S(1)} %get-tuple-element.390, u32[4096]{0:T(1024)S(1)} %broadcast_clamp_fusion.3), kind=kCustom, calls=%fused_computation.clone.clone.1 | custom fusion | bytes 49152 | tf_op jit(solution)/shard_map/jit(searchsorted)/jit(_searchsorted_scan_impl)/vmap(jit(_searchsorted_scan_impl))/while/body/eval_jaxpr/gather | solution.py:72
  83.8 23.0 %gather_fusion.1 = s32[4096]{0:T(1024)S(1)} fusion(s32[4096]{0:T(1024)S(1)} %get-tuple-element.390, u32[4096]{0:T(1024)S(1)} %broadcast_clamp_fusion.3), kind=kCustom, calls=%fused_computation.clone.clone.1 | custom fusion | bytes 49152 | tf_op jit(solution)/shard_map/jit(searchsorted)/jit(_searchsorted_scan_impl)/vmap(jit(_searchsorted_scan_impl))/while/body/eval_jaxpr/gather | solution.py:72
  106.9 23.0 %gather_fusion.1 = s32[4096]{0:T(1024)S(1)} fusion(s32[4096]{0:T(1024)S(1)} %get-tuple-element.390, u32[4096]{0:T(1024)S(1)} %broadcast_clamp_fusion.3), kind=kCustom, calls=%fused_computation.clone.clone.1 | custom fusion | bytes 49152 | tf_op jit(solution)/shard_map/jit(searchsorted)/jit(_searchsorted_scan_impl)/vmap(jit(_searchsorted_scan_impl))/while/body/eval_jaxpr/gather | solution.py:72
  130.0 23.0 %gather_fusion.1 = s32[4096]{0:T(1024)S(1)} fusion(s32[4096]{0:T(1024)S(1)} %get-tuple-element.390, u32[4096]{0:T(1024)S(1)} %broadcast_clamp_fusion.3), kind=kCustom, calls=%fused_computation.clone.clone.1 | custom fusion | bytes 49152 | tf_op jit(solution)/shard_map/jit(searchsorted)/jit(_searchsorted_scan_impl)/vmap(jit(_searchsorted_scan_impl))/while/body/eval_jaxpr/gather | solution.py:72
  153.2 23.0 %gather_fusion.1 = s32[4096]{0:T(1024)S(1)} fusion(s32[4096]{0:T(1024)S(1)} %get-tuple-element.390, u32[4096]{0:T(1024)S(1)} %broadcast_clamp_fusion.3), kind=kCustom, calls=%fused_computation.clone.clone.1 | custom fusion | bytes 49152 | tf_op jit(solution)/shard_map/jit(searchsorted)/jit(_searchsorted_scan_impl)/vmap(jit(_searchsorted_scan_impl))/while/body/eval_jaxpr/gather | solution.py:72
  176.3 23.0 %gather_fusion.1 = s32[4096]{0:T(1024)S(1)} fusion(s32[4096]{0:T(1024)S(1)} %get-tuple-element.390, u32[4096]{0:T(1024)S(1)} %broadcast_clamp_fusion.3), kind=kCustom, calls=%fused_computation.clone.clone.1 | custom fusion | bytes 49152 | tf_op jit(solution)/shard_map/jit(searchsorted)/jit(_searchsorted_scan_impl)/vmap(jit(_searchsorted_scan_impl))/while/body/eval_jaxpr/gather | solution.py:72
  199.4 23.0 %gather_fusion.1 = s32[4096]{0:T(1024)S(1)} fusion(s32[4096]{0:T(1024)S(1)} %get-tuple-element.390, u32[4096]{0:T(1024)S(1)} %broadcast_clamp_fusion.3), kind=kCustom, calls=%fused_computation.clone.clone.1 | custom fusion | bytes 49152 | tf_op jit(solution)/shard_map/jit(searchsorted)/jit(_searchsorted_scan_impl)/vmap(jit(_searchsorted_scan_impl))/while/body/eval_jaxpr/gather | solution.py:72
  222.5 23.0 %gather_fusion.1 = s32[4096]{0:T(1024)S(1)} fusion(s32[4096]{0:T(1024)S(1)} %get-tuple-element.390, u32[4096]{0:T(1024)S(1)} %broadcast_clamp_fusion.3), kind=kCustom, calls=%fused_computation.clone.clone.1 | custom fusion | bytes 49152 | tf_op jit(solution)/shard_map/jit(searchsorted)/jit(_searchsorted_scan_impl)/vmap(jit(_searchsorted_scan_impl))/while/body/eval_jaxpr/gather | solution.py:72
  245.7 23.0 %gather_fusion.1 = s32[4096]{0:T(1024)S(1)} fusion(s32[4096]{0:T(1024)S(1)} %get-tuple-element.390, u32[4096]{0:T(1024)S(1)} %broadcast_clamp_fusion.3), kind=kCustom, calls=%fused_computation.clone.clone.1 | custom fusion | bytes 49152 | tf_op jit(solution)/shard_map/jit(searchsorted)/jit(_searchsorted_scan_impl)/vmap(jit(_searchsorted_scan_impl))/while/body/eval_jaxpr/gather | solution.py:72
  268.8 23.0 %gather_fusion.1 = s32[4096]{0:T(1024)S(1)} fusion(s32[4096]{0:T(1024)S(1)} %get-tuple-element.390, u32[4096]{0:T(1024)S(1)} %broadcast_clamp_fusion.3), kind=kCustom, calls=%fused_computation.clone.clone.1 | custom fusion | bytes 49152 | tf_op jit(solution)/shard_map/jit(searchsorted)/jit(_searchsorted_scan_impl)/vmap(jit(_searchsorted_scan_impl))/while/body/eval_jaxpr/gather | solution.py:72
  291.9 23.0 %gather_fusion.1 = s32[4096]{0:T(1024)S(1)} fusion(s32[4096]{0:T(1024)S(1)} %get-tuple-element.390, u32[4096]{0:T(1024)S(1)} %broadcast_clamp_fusion.3), kind=kCustom, calls=%fused_computation.clone.clone.1 | custom fusion | bytes 49152 | tf_op jit(solution)/shard_map/jit(searchsorted)/jit(_searchsorted_scan_impl)/vmap(jit(_searchsorted_scan_impl))/while/body/eval_jaxpr/gather | solution.py:72
  315.1 23.0 %gather_fusion.1 = s32[4096]{0:T(1024)S(1)} fusion(s32[4096]{0:T(1024)S(1)} %get-tuple-element.390, u32[4096]{0:T(1024)S(1)} %broadcast_clamp_fusion.3), kind=kCustom, calls=%fused_computation.clone.clone.1 | custom fusion | bytes 49152 | tf_op jit(solution)/shard_map/jit(searchsorted)/jit(_searchsorted_scan_impl)/vmap(jit(_searchsorted_scan_impl))/while/body/eval_jaxpr/gather | solution.py:72
  338.2 2.1 reshape.192
  340.4 15.5 %scatter_custom_fusion = s32[4096]{0:T(1024)S(1)} fusion(s32[4096]{0:T(1024)S(1)} %get-tuple-element.256, s32[4096]{0:T(1024)S(1)} %convert_subtract_fusion, s32[]{:T(128)} %constant.136.clone.1), kind=kCustom, calls=%fused_computation.51 | custom fusion | bytes 16388 | tf_op jit(solution)/shard_map/scatter | solution.py:74
  356.0 2.3 copy.69
  358.5 1.0 copy.50
  359.7 180.2 %while.38 = (s32[]{:T(128)}, f32[27,64,64]{2,0,1:T(8,128)S(1)}, bf16[3,8,4,64,64]{4,3,2,1,0:T(8,128)(2,1)}, s32[64]{0:T(128)S(1)}, s32[64,4]{0,1:T(4,128)S(1)}, ...) while((s32[]{:T(128)}, f32[27,64,64]{2,0,1:T(8,128)S(1)}, ...), condition=%wide.region_5.6_spmd, body=%wide.region_4.5_spmd.sunk | while | flops 120784584 | bytes 33826512 | solution.py:121
  373.1 1.1 fusion.46
  374.5 7.9 %broadcast_multiply_fusion.7 = f32[8,8,8,4,16,64]{5,4,3,2,1,0:T(8,128)} fusion(f32[8,4,16,64]{3,2,1,0:T(8,128)S(1)} %get-tuple-element.364, f32[8,8,4,16,64]{4,3,2,1,0:T(8,128)S(1)} %broadcast_multiply_fusion.6), kind=kLoop, calls=%fused_computation.10.clone.1 | loop fusion | flops 2097152 | bytes 9568256 | tf_op jit(solution)/shard_map/while/body/eval_jaxpr/mul | solution.py:15
  382.5 9.4 %fusion.48 = bf16[512,4,16,64]{3,2,1,0:T(8,128)(2,1)} fusion(f32[8,8,8,4,16,64]{5,4,3,2,1,0:T(8,128)} %broadcast_multiply_fusion.7, f32[4,16]{1,0:T(4,128)S(1)} %fusion.47), kind=kLoop, calls=%fused_computation.7.clone.1 | loop fusion | flops 4194304 | bytes 12583168 | tf_op jit(solution)/shard_map/while/body/eval_jaxpr/convert_element_type | solution.py:19
  392.2 2.0 gather_fusion
  394.2 20.6 %fusion.49 = f32[27,64,64]{2,0,1:T(8,128)S(1)} fusion(f32[27,64,64]{2,0,1:T(8,128)S(1)} %get-tuple-element.407, s32[]{:T(128)S(6)} %select_n.100, bf16[16,4,27,512]{3,2,1,0:T(8,128)(2,1)} %bitcast.141, pred[16,4]{1,0:T(8,128)(4,1)S(1)} %compare_and_fusion.2, bf16[512,4,16,64]{3,2,1,0:T(8,128)(2,1)} %fusion.48), kind=kOutput, calls=%fused_computation.15.clone.1 | convolution fusion | flops 114130944 | bytes 6227972 | tf_op jit(solution)/shard_map/while/body/eval_jaxpr/cnkv,vkns->cns/dot_general | solution.py:116
  414.8 1.1 fusion.46
  416.2 7.9 %broadcast_multiply_fusion.7 = f32[8,8,8,4,16,64]{5,4,3,2,1,0:T(8,128)} fusion(f32[8,4,16,64]{3,2,1,0:T(8,128)S(1)} %get-tuple-element.364, f32[8,8,4,16,64]{4,3,2,1,0:T(8,128)S(1)} %broadcast_multiply_fusion.6), kind=kLoop, calls=%fused_computation.10.clone.1 | loop fusion | flops 2097152 | bytes 9568256 | tf_op jit(solution)/shard_map/while/body/eval_jaxpr/mul | solution.py:15
  424.2 9.4 %fusion.48 = bf16[512,4,16,64]{3,2,1,0:T(8,128)(2,1)} fusion(f32[8,8,8,4,16,64]{5,4,3,2,1,0:T(8,128)} %broadcast_multiply_fusion.7, f32[4,16]{1,0:T(4,128)S(1)} %fusion.47), kind=kLoop, calls=%fused_computation.7.clone.1 | loop fusion | flops 4194304 | bytes 12583168 | tf_op jit(solution)/shard_map/while/body/eval_jaxpr/convert_element_type | solution.py:19
  433.8 2.0 gather_fusion
  435.9 20.6 %fusion.49 = f32[27,64,64]{2,0,1:T(8,128)S(1)} fusion(f32[27,64,64]{2,0,1:T(8,128)S(1)} %get-tuple-element.407, s32[]{:T(128)S(6)} %select_n.100, bf16[16,4,27,512]{3,2,1,0:T(8,128)(2,1)} %bitcast.141, pred[16,4]{1,0:T(8,128)(4,1)S(1)} %compare_and_fusion.2, bf16[512,4,16,64]{3,2,1,0:T(8,128)(2,1)} %fusion.48), kind=kOutput, calls=%fused_computation.15.clone.1 | convolution fusion | flops 114130944 | bytes 6227972 | tf_op jit(solution)/shard_map/while/body/eval_jaxpr/cnkv,vkns->cns/dot_general | solution.py:116
  456.4 1.1 fusion.46
  457.8 7.9 %broadcast_multiply_fusion.7 = f32[8,8,8,4,16,64]{5,4,3,2,1,0:T(8,128)} fusion(f32[8,4,16,64]{3,2,1,0:T(8,128)S(1)} %get-tuple-element.364, f32[8,8,4,16,64]{4,3,2,1,0:T(8,128)S(1)} %broadcast_multiply_fusion.6), kind=kLoop, calls=%fused_computation.10.clone.1 | loop fusion | flops 2097152 | bytes 9568256 | tf_op jit(solution)/shard_map/while/body/eval_jaxpr/mul | solution.py:15
  465.8 9.4 %fusion.48 = bf16[512,4,16,64]{3,2,1,0:T(8,128)(2,1)} fusion(f32[8,8,8,4,16,64]{5,4,3,2,1,0:T(8,128)} %broadcast_multiply_fusion.7, f32[4,16]{1,0:T(4,128)S(1)} %fusion.47), kind=kLoop, calls=%fused_computation.7.clone.1 | loop fusion | flops 4194304 | bytes 12583168 | tf_op jit(solution)/shard_map/while/body/eval_jaxpr/convert_element_type | solution.py:19
  475.5 2.0 gather_fusion
  477.5 20.6 %fusion.49 = f32[27,64,64]{2,0,1:T(8,128)S(1)} fusion(f32[27,64,64]{2,0,1:T(8,128)S(1)} %get-tuple-element.407, s32[]{:T(128)S(6)} %select_n.100, bf16[16,4,27,512]{3,2,1,0:T(8,128)(2,1)} %bitcast.141, pred[16,4]{1,0:T(8,128)(4,1)S(1)} %compare_and_fusion.2, bf16[512,4,16,64]{3,2,1,0:T(8,128)(2,1)} %fusion.48), kind=kOutput, calls=%fused_computation.15.clone.1 | convolution fusion | flops 114130944 | bytes 6227972 | tf_op jit(solution)/shard_map/while/body/eval_jaxpr/cnkv,vkns->cns/dot_general | solution.py:116
  498.1 1.1 fusion.46
  499.5 7.9 %broadcast_multiply_fusion.7 = f32[8,8,8,4,16,64]{5,4,3,2,1,0:T(8,128)} fusion(f32[8,4,16,64]{3,2,1,0:T(8,128)S(1)} %get-tuple-element.364, f32[8,8,4,16,64]{4,3,2,1,0:T(8,128)S(1)} %broadcast_multiply_fusion.6), kind=kLoop, calls=%fused_computation.10.clone.1 | loop fusion | flops 2097152 | bytes 9568256 | tf_op jit(solution)/shard_map/while/body/eval_jaxpr/mul | solution.py:15
  507.5 9.4 %fusion.48 = bf16[512,4,16,64]{3,2,1,0:T(8,128)(2,1)} fusion(f32[8,8,8,4,16,64]{5,4,3,2,1,0:T(8,128)} %broadcast_multiply_fusion.7, f32[4,16]{1,0:T(4,128)S(1)} %fusion.47), kind=kLoop, calls=%fused_computation.7.clone.1 | loop fusion | flops 4194304 | bytes 12583168 | tf_op jit(solution)/shard_map/while/body/eval_jaxpr/convert_element_type | solution.py:19
  517.1 2.0 gather_fusion
  519.2 20.6 %fusion.49 = f32[27,64,64]{2,0,1:T(8,128)S(1)} fusion(f32[27,64,64]{2,0,1:T(8,128)S(1)} %get-tuple-element.407, s32[]{:T(128)S(6)} %select_n.100, bf16[16,4,27,512]{3,2,1,0:T(8,128)(2,1)} %bitcast.141, pred[16,4]{1,0:T(8,128)(4,1)S(1)} %compare_and_fusion.2, bf16[512,4,16,64]{3,2,1,0:T(8,128)(2,1)} %fusion.48), kind=kOutput, calls=%fused_computation.15.clone.1 | convolution fusion | flops 114130944 | bytes 6227972 | tf_op jit(solution)/shard_map/while/body/eval_jaxpr/cnkv,vkns->cns/dot_general | solution.py:116
  540.0 1.0 broadcast_multiply_fusion.2
  542.6 1.0 convolution_bitcast_fusion
  543.5 1.0 fusion.33
  544.5 111.1 %all-reduce = (f32[8]{0:T(128)S(1)}, f32[8,8]{0,1:T(8,128)S(1)}) all-reduce(f32[8]{0:T(128)S(1)} %convolution_bitcast_fusion, f32[8,8]{0,1:T(8,128)S(1)} %fusion.33), channel_id=1, replica_groups=mesh['slab'=32,'grp'=16] {'slab','grp'}, use_global_device_ids=true, to_apply=%region_6.7 | all-reduce | flops 72 | bytes 576 | tf_op jit(solution)/shard_map/psum | solution.py:130
  656.4 0.7 cholesky.19
  657.3 0.6 compare_reduce_fusion
  657.9 0.6 select_select_fusion.2
  658.6 0.7 fusion.31
  659.3 0.7 fusion.30
  660.1 0.7 fusion.32
  711.9 0.7 fusion.24
  713.4 12.8 %scatter_custom_fusion.1 = f32[8,8192]{0,1:T(8,128)} fusion(s32[4096]{0:T(1024)S(1)} %compare_select_fusion.1, f32[4096,8]{1,0:T(8,128)S(1)} %copy.59, f32[]{:T(128)} %constant.134.clone.1), kind=kCustom, calls=%fused_computation.35 | custom fusion | bytes 262148 | tf_op jit(solution)/shard_map/scatter | solution.py:79
  726.2 2.9 copy.60
  729.1 0.7 reshape.198
  729.8 13.1 %all_to_all.10 = f32[32,1,2048]{2,1,0:T(1,128)S(1)} all-to-all(f32[32,1,2048]{2,1,0:T(1,128)S(1)} %reshape.198), channel_id=1, replica_groups=mesh['slab'=32,'grp'=16] {'slab'}, dimensions={0} | all-to-all | bytes 524288 | tf_op jit(solution)/shard_map/all_to_all | solution.py:137
  743.5 1.3 reduce.6
  744.7 0.7 reshape.199
  745.4 1.3 copy.61
  747.2 21.1 %all_to_all.11 = f32[16,1,4096]{2,1,0:T(1,128)S(1)} all-to-all(f32[16,1,4096]{2,1,0:T(1,128)S(1)} %reshape.200), channel_id=1, replica_groups=mesh['slab'=32,'grp'=16] {'grp'}, dimensions={0} | all-to-all | bytes 524288 | tf_op jit(solution)/shard_map/all_to_all | solution.py:136
  768.4 1.3 reduce.7
  770.0 0.9 copy.62
  770.9 2.3 reshape.128
  (140 shorter events, 8.4 us)
Async XLA Ops:
  7.2 7.3 copy-start
  7.2 348.8 %all-gather.2.cloned.1.call-start = ((), (), s32[]{:S(2)}) async-start(), calls=%async_computation.2 | async-start | bytes 2228224 | tf_op jit(solution)/shard_map/all_gather | solution.py:104
  37.5 300.7 %copy-start.2 = (bf16[3,8,4,4096]{3,2,1,0:T(4,128)(2,1)S(1)}, bf16[3,8,4,4096]{3,2,1,0:T(4,128)(2,1)}, u32[]{:S(2)}) copy-start(bf16[3,8,4,4096]{3,2,1,0:T(4,128)(2,1)} %param.12) | copy-start | bytes 2359300
  338.2 2.2 copy-start.3
  358.5 1.2 copy-start.5
  358.5 1.2 copy-start.7
  541.0 0.8 copy-start.4
  541.0 1.2 copy-start.1
  711.9 14.2 %copy-start.6 = (f32[8]{0:T(128)}, f32[8]{0:T(128)S(1)}, u32[]{:S(2)}) copy-start(f32[8]{0:T(128)S(1)} %stack.35) | copy-start | bytes 100
Sparse Core Ops, SparseCore 0:
  10.1 69.3 all-gather.1
where the time goes:
time: 783 us; the launch traced here: 780 us
  local copies, waits for them, and re-layouts  382 us (49%)
  blocking collectives  145 us (19%)
  other arithmetic  87.6 us (11%)
  matrix products  84.8 us (11%)
  between operations  65.5 us (8%)
  loops' own time  14.6 us (2%)
    gather x13, local copies, waits for them, and re-layouts, place_slots(): run_start = jnp.searchsorted(ordered, ordered, side='left')  299 us
    psum x1, blocking collectives, body(): hessian, gradient = lax.psum((hess_local, grad_local), ('slab', 'grp'))  111 us
    dot_general x4, matrix products, interp_step(): jnp.einsum('cnkv,vkns->cns', picked, tile_set, preferred_element_type=jnp...  82.2 us
    convert_element_type x4, other arithmetic, build_tiles(): return (product * keep_mask[None, :, :, None]).astype(jnp.bfloat16)  37.5 us
    mul x4, other arithmetic, build_tiles(): product = product * along_x[None, None, :]  31.7 us
    gather x1, local copies, waits for them, and re-layouts, place_slots(): ordered = destination[permutation]  23 us
    all_to_all x1, blocking collectives, body(): lax.all_to_all(lax.all_to_all(placed, 'slab', split_axis=1, concat_axis=1...  21.1 us
  transfers between devices with their start and end apart: 1, of which 0 were waited for; matrix products, arithmetic and copies ran while one was open for 44% of the time, Pallas kernels for 0%

commit v1 on v0

v1 whole, which is shorter than its diff:
```python
import functools

import jax
import jax.numpy as jnp
from jax import lax
from jax.experimental import pallas as pl
from jax.experimental.pallas import tpu as pltpu
from jax.sharding import PartitionSpec as P

MESH = pl.DeviceIdType.MESH
F32 = jnp.float32
BF16 = jnp.bfloat16
DAMPING = 0.05

PARAMS = 8
COMPS = 3
CHANNELS = 27
ROWS = 32
BLOCKS = 4
PACKED = 112
BLK = 512
HALF = 256
SLOTS = 4
CAP = 16
GRP = 16
SLAB = 32
SUBSETS = 4096
TILES = 32
CHUNK = 256
CHUNKS = 16
PEERS = 512
HIGH = 64


def iota(shape, axis):
    return lax.broadcasted_iota(jnp.int32, shape, axis)


def split_two(value):
    upper = value.astype(BF16).astype(F32)
    return upper, (value - upper).astype(BF16).astype(F32)


def swap_chunks(value):
    sub, lane = iota((8, 128), 0), iota((8, 128), 1)
    for bit in range(3):
        step = 1 << bit
        sub_bit, lane_bit = (sub >> bit) & 1, (lane >> (4 + bit)) & 1
        upward = pltpu.roll(pltpu.roll(value, 16 * step, 1), 8 - step, 0)
        downward = pltpu.roll(pltpu.roll(value, 128 - 16 * step, 1), step, 0)
        value = jnp.where(sub_bit == lane_bit, value, jnp.where(sub_bit == 0, upward, downward))
    return value


def kernel(
    ids_ref, live_ref, fields_ref, spline_hbm, meas_ref, conf_ref, own_ref,
    out_ref, upd_ref,
    spline_ref, spline_sem, land, store, tiles, sp32, carry, upper_ref, unpack_ref,
    scatter_b, scatter_m, scatter_a, early_acc, sens, resid, norm_l, norm_r,
    red1, red2, early_out, early1, early2_out, early2, late_out, late1, late2_out, late2, flip,
    ag_send, ag_recv, r1s, r1r, r2s, r2r, e1s, e1r, e2s, e2r, d1s, d1r, d2s, d2r,
):
    me_s = lax.axis_index("slab")
    me_g = lax.axis_index("grp")
    right, left = lax.rem(me_g + 1, GRP), lax.rem(me_g + GRP - 1, GRP)

    barrier = pltpu.get_barrier_semaphore()

    @pl.loop(1, GRP)
    def _(j):
        pl.semaphore_signal(barrier, inc=1, device_id=(me_s, lax.rem(me_g + j, GRP)), device_id_type=MESH)

    @pl.loop(1, SLAB)
    def _(j):
        pl.semaphore_signal(barrier, inc=1, device_id=(lax.rem(me_s + j, SLAB), me_g), device_id_type=MESH)

    spline_copy = pltpu.make_async_copy(spline_hbm, spline_ref, spline_sem)
    spline_copy.start()

    row = iota((PACKED, CHANNELS), 0)
    channel = iota((PACKED, CHANNELS), 1)
    packed = None
    for j in range(BLOCKS):
        new = row - CHANNELS * j
        source = jnp.where(new < 24, 3 + 3 * (new & 7) + (new >> 3), new - 24)
        pick = (channel == source) & (new >= 0) & (new < CHANNELS)
        part = jnp.dot(
            jnp.where(pick, 1.0, 0.0).astype(BF16), fields_ref[:, j * BLK:(j + 1) * BLK], preferred_element_type=F32
        )
        packed = part if packed is None else packed + part
    packed = packed.astype(BF16)
    land[0, me_g] = packed[:, :HALF]
    land[1, me_g] = packed[:, HALF:]

    row, col = iota((CHUNK, CHUNK + 128), 0), iota((CHUNK, CHUNK + 128), 1)
    upper_ref[...] = jnp.where((row < col) | (col >= CHUNK), 1.0, 0.0).astype(BF16)
    row, col = iota((BLOCKS * ROWS, PACKED), 0), iota((BLOCKS * ROWS, PACKED), 1)
    unpack = jnp.zeros((BLOCKS * ROWS, PACKED), F32)
    for j in range(BLOCKS):
        inside = (row >= ROWS * j) & (row < ROWS * j + CHANNELS)
        unpack = jnp.where(inside & (col == row - (ROWS - CHANNELS) * j), 1.0, unpack)
    unpack_ref[...] = unpack.astype(BF16)
    carry[...] = jnp.zeros_like(carry)
    early_acc[...] = jnp.zeros_like(early_acc)
    late_out[...] = jnp.zeros_like(late_out)
    norm_r[...] = jnp.zeros_like(norm_r)

    def ring(direction, i, h, slot, target):
        return pltpu.make_async_remote_copy(
            src_ref=land.at[h, slot], dst_ref=land.at[h, slot],
            send_sem=ag_send.at[direction, i, h], recv_sem=ag_recv.at[direction, i, h],
            device_id=(me_s, target), device_id_type=MESH,
        )

    def unpack_slot(h, slot):
        rows = jnp.dot(unpack_ref[...], land[h, slot], preferred_element_type=F32).astype(BF16)
        store[h, pl.ds(BLOCKS * slot, BLOCKS)] = rows.reshape(BLOCKS, ROWS, HALF)

    def build_tile(t):
        lanes = pl.ds(pl.multiple_of(t * 128, 128), 128)
        for axis in range(3):
            part = spline_ref[axis, :, :, lanes].astype(F32)
            for e in range(8):
                sp32[axis, e * 4:(e + 1) * 4, :] = part[e]
        live_row = jnp.where(iota((8, 128), 1) < 64, live_ref[2 * t], live_ref[2 * t + 1])
        for k in range(SLOTS):
            along_z = sp32[0, pl.ds(k, 8, stride=4), :]
            along_y = sp32[1, pl.ds(k, 8, stride=4), :]
            along_x = sp32[2, pl.ds(k, 8, stride=4), :]
            along_z = jnp.where(live_row > k, along_z, 0.0)
            for z in range(8):
                face = along_z[z:z + 1, :] * along_y
                cells = (face[:, None, :] * along_x[None, :, :]).reshape(64, 128)
                start = (z // 4) * 1024 + k * HALF + (z % 4) * 64
                tiles[t, start:start + 64, :] = cells.astype(BF16)

    def place_chunk(j):
        lanes = pl.ds(pl.multiple_of(j * CHUNK, CHUNK), CHUNK)
        owner = own_ref[:, lanes]
        onehot = jnp.where(iota((PEERS, CHUNK), 0) == owner, 1.0, 0.0)
        counted = jnp.dot(onehot.astype(BF16), upper_ref[...], preferred_element_type=F32)
        before = carry[...]
        rank = jnp.sum(
            onehot * (counted[:, :CHUNK] + jnp.concatenate([before, before], axis=1)), axis=0, keepdims=True
        )
        carry[...] = before + counted[:, CHUNK:]
        low = ((owner >> 4) & 7) * CAP + rank.astype(jnp.int32)
        high = (owner & 15) * 4 + (owner >> 7)
        column = jnp.where(iota((128, CHUNK), 0) == low, 1.0, 0.0).T.astype(BF16)
        scatter_b[lanes, :] = column
        mask = jnp.where(iota((HIGH, CHUNK), 0) == high, 1.0, 0.0)
        scatter_m[:, lanes] = mask.astype(BF16)
        pieces = []
        for value in [meas_ref[c:c + 1, lanes] for c in range(COMPS)] + [conf_ref[:, lanes]]:
            pieces.append(split_two(value))
        stacked = jnp.concatenate(
            [(mask * pieces[c][part]).astype(BF16) for part in range(2) for c in range(4)], axis=0
        )
        early_acc[...] += jnp.dot(stacked, column, preferred_element_type=F32)

    pl.semaphore_wait(barrier, GRP + SLAB - 2)

    @pl.loop(0, CHUNKS)
    def _(j):
        i, h = j // 2, j % 2
        back, ahead = lax.rem(me_g + GRP - i, GRP), lax.rem(me_g + i, GRP)

        @pl.when(i > 0)
        def _():
            ring(0, i - 1, h, back, right).wait_recv()
            ring(1, i - 1, h, ahead, left).wait_recv()

        @pl.when((i < 7) | (h == 0))
        def _():
            ring(0, i, h, back, right).start()

        @pl.when((i < 7) | (h == 1))
        def _():
            ring(1, i, h, ahead, left).start()

        @pl.when(j == 0)
        def _():
            spline_copy.wait()

        unpack_slot(h, back)
        unpack_slot(h, ahead)
        build_tile(2 * j)
        build_tile(2 * j + 1)
        place_chunk(j)

    total = early_acc[0:4 * HIGH, :] + early_acc[4 * HIGH:, :]
    for c in range(4):
        for g in range(GRP):
            early_out[16 * g + 4 * c:16 * g + 4 * c + 4, :] = total[HIGH * c + 4 * g:HIGH * c + 4 * g + 4, :]

    opposite = lax.rem(me_g + 8, GRP)
    ring(0, 7, 0, opposite, right).wait_recv()
    ring(1, 7, 1, opposite, left).wait_recv()
    unpack_slot(0, opposite)
    unpack_slot(1, opposite)

    def group_copy(source, landing, send, recv, j, arriving):
        peer = lax.rem(me_g + j, GRP)
        origin = peer if arriving else me_g
        return pltpu.make_async_remote_copy(
            src_ref=source.at[pl.ds(pl.multiple_of(16 * peer, 16), 16)],
            dst_ref=landing.at[pl.ds(pl.multiple_of(16 * origin, 16), 16)],
            send_sem=send.at[peer], recv_sem=recv.at[origin],
            device_id=(me_s, peer), device_id_type=MESH,
        )

    def slab_copy(source, landing, send, recv, j, arriving):
        peer = lax.rem(me_s + j, SLAB)
        origin = peer if arriving else me_s
        return pltpu.make_async_remote_copy(
            src_ref=source.at[peer], dst_ref=landing.at[origin],
            send_sem=send.at[peer], recv_sem=recv.at[origin],
            device_id=(peer, me_g), device_id_type=MESH,
        )

    def reduce_copy(buffer, send, recv, j, arriving, along_group):
        size = GRP if along_group else SLAB
        mine = me_g if along_group else me_s
        peer = lax.rem(mine + j, size)
        origin = peer if arriving else mine
        return pltpu.make_async_remote_copy(
            src_ref=buffer.at[origin], dst_ref=buffer.at[origin],
            send_sem=send.at[peer], recv_sem=recv.at[origin],
            device_id=(me_s, peer) if along_group else (peer, me_g), device_id_type=MESH,
        )

    @pl.loop(1, GRP)
    def _(j):
        group_copy(early_out, early1, e1s, e1r, j, False).start()

    mine = pl.ds(pl.multiple_of(16 * me_g, 16), 16)
    early1[mine, :] = early_out[mine, :]

    @pl.loop(0, TILES)
    def _(t):
        lanes = pl.ds(pl.multiple_of(t * 128, 128), 128)
        rows = []
        for part in range(2):
            rows.append(
                jnp.concatenate(
                    [store[h, ids_ref[k, 2 * t + part]] for h in range(2) for k in range(SLOTS)], axis=1
                )
            )
        both = jnp.dot(jnp.concatenate(rows, axis=0), tiles[t], preferred_element_type=F32)
        lane = iota((ROWS, 128), 1)
        modelled = jnp.where(lane < 64, both[:ROWS], both[ROWS:])
        weight = conf_ref[:, lanes]
        residual = meas_ref[:, lanes] - modelled[24:27]
        sens[:, lanes] = modelled[:24]
        resid[0:3, lanes] = residual
        upper, lower = split_two(modelled[:24])
        norm_l[0:24, lanes] = upper
        norm_l[24:48, lanes] = lower
        weighted = [split_two(modelled[8 * c:8 * c + 8] * weight) for c in range(COMPS)]
        right_side = split_two(residual * weight)
        for part in range(2):
            for c in range(COMPS):
                start = 64 * part + 16 * c
                norm_r[start:start + 8, lanes] = weighted[c][part]
                norm_r[start + 8:start + 9, lanes] = right_side[part][c:c + 1]

    gram = lax.dot_general(
        norm_l[...].astype(BF16), norm_r[...].astype(BF16), (((1,), (1,)), ((), ())), preferred_element_type=F32
    )
    gram = gram[:24] + gram[24:]
    gram = gram + pltpu.roll(gram, 64, 1)
    normal = gram[:8] + pltpu.roll(gram[8:16], 112, 1) + pltpu.roll(gram[16:24], 96, 1)
    sub, lane = iota((8, 128), 0), iota((8, 128), 1)
    normal = jnp.where(lane < 16, normal, 0.0)
    for shift in (16, 32, 64):
        normal = normal + pltpu.roll(normal, shift, 1)
    own_chunk = (lane >> 4) == sub
    red1[me_g] = jnp.sum(jnp.where(own_chunk, normal, 0.0), axis=0, keepdims=True)

    @pl.loop(1, GRP)
    def _(j):
        reduce_copy(red1, r1s, r1r, j, False, True).start()

    @pl.loop(1, GRP)
    def _(j):
        group_copy(early_out, early1, e1s, e1r, j, True).wait_recv()

    def turn(landing, outgoing, comps):
        for c in range(comps):
            for upper_part in range(4):
                for side in range(2):
                    block = landing[pl.ds(128 * side + 4 * c + upper_part, 8, stride=16), :]
                    start = 64 * upper_part + 8 * (4 * side + c)
                    flip[start:start + 8, :] = swap_chunks(block)
        for upper_part in range(4):
            for lower_part in range(8):
                outgoing[8 * upper_part + lower_part] = flip[pl.ds(64 * upper_part + lower_part, 8, stride=8), :]

    turn(early1, early2_out, 4)

    @pl.loop(1, GRP)
    def _(j):
        reduce_copy(red1, r1s, r1r, j, True, True).wait_recv()

    red2[me_s] = jnp.sum(red1[...], axis=0)

    @pl.loop(1, SLAB)
    def _(j):
        reduce_copy(red2, r2s, r2r, j, False, False).start()

    @pl.loop(1, SLAB)
    def _(j):
        slab_copy(early2_out, early2, e2s, e2r, j, False).start()

    early2[me_s] = early2_out[me_s]

    @pl.loop(1, SLAB)
    def _(j):
        reduce_copy(red2, r2s, r2r, j, True, False).wait_recv()

    system = jnp.where(own_chunk, jnp.sum(red2[...], axis=0), 0.0)
    for shift in (16, 32, 64):
        system = system + pltpu.roll(system, shift, 1)
    column = lane & 15
    system = jnp.where(column == sub, system * (1.0 + DAMPING), system)
    for i in range(PARAMS):
        factor = system[:, i:i + 1]
        pivot_row = system[i:i + 1, :] / system[i:i + 1, i:i + 1]
        system = jnp.where(sub == i, pivot_row, system - factor * pivot_row)
    update = system[:, 8:9]
    flat = jnp.sum(jnp.where(lane == sub, update, 0.0), axis=0, keepdims=True)
    upd_ref[...] = flat[:, :PARAMS]

    for q in range(8):
        lanes = slice(512 * q, 512 * (q + 1))
        mask = scatter_m[:, lanes].astype(F32)
        for c in range(COMPS):
            predicted = jnp.sum(sens[8 * c:8 * c + 8, lanes] * update, axis=0, keepdims=True)
            remaining = split_two(resid[c:c + 1, lanes] - predicted)
            for part in range(2):
                start = HIGH * (3 * part + c)
                scatter_a[start:start + HIGH, lanes] = (mask * remaining[part]).astype(BF16)
    placed = jnp.dot(scatter_a[...], scatter_b[...], preferred_element_type=F32)
    placed = placed[:3 * HIGH] + placed[3 * HIGH:]
    for c in range(COMPS):
        for g in range(GRP):
            late_out[16 * g + 4 * c:16 * g + 4 * c + 4, :] = placed[HIGH * c + 4 * g:HIGH * c + 4 * g + 4, :]

    @pl.loop(1, GRP)
    def _(j):
        group_copy(late_out, late1, d1s, d1r, j, False).start()

    late1[mine, :] = late_out[mine, :]

    @pl.loop(1, GRP)
    def _(j):
        group_copy(late_out, late1, d1s, d1r, j, True).wait_recv()

    turn(late1, late2_out, 3)

    @pl.loop(1, SLAB)
    def _(j):
        slab_copy(late2_out, late2, d2s, d2r, j, False).start()

    late2[me_s] = late2_out[me_s]

    @pl.loop(1, SLAB)
    def _(j):
        slab_copy(early2_out, early2, e2s, e2r, j, True).wait_recv()

    @pl.loop(1, SLAB)
    def _(j):
        slab_copy(late2_out, late2, d2s, d2r, j, True).wait_recv()

    for first in range(0, SLAB, 8):
        for side in range(2):
            def rows_of(ref, c):
                return jnp.concatenate([ref[first + n, 4 * side + c:4 * side + c + 1, :] for n in range(8)], axis=0)

            confidence = rows_of(early2, 3)
            squares = jnp.zeros_like(confidence)
            results = []
            late_rows = [rows_of(late2, c) for c in range(COMPS)]
            for c in range(COMPS):
                results.append(rows_of(early2, c) - late_rows[c])
            for c in range(COMPS):
                results.append(confidence * late_rows[c])
                squares = squares + late_rows[c] * late_rows[c]
            results.append(confidence)
            results.append(confidence * squares)
            for r in range(8):
                flip[8 * r:8 * r + 8, :] = results[r]
            for n in range(8):
                start = 256 * (first + n) + 128 * side
                out_ref[:, start:start + 128] = flip[pl.ds(n, 8, stride=8), :]

    @pl.loop(0, CHUNKS)
    def _(j):
        i, h = j // 2, j % 2
        back, ahead = lax.rem(me_g + GRP - i, GRP), lax.rem(me_g + i, GRP)

        @pl.when((i < 7) | (h == 0))
        def _():
            ring(0, i, h, back, right).wait_send()

        @pl.when((i < 7) | (h == 1))
        def _():
            ring(1, i, h, ahead, left).wait_send()

    @pl.loop(1, GRP)
    def _(j):
        group_copy(early_out, early1, e1s, e1r, j, False).wait_send()
        group_copy(late_out, late1, d1s, d1r, j, False).wait_send()
        reduce_copy(red1, r1s, r1r, j, False, True).wait_send()

    @pl.loop(1, SLAB)
    def _(j):
        slab_copy(early2_out, early2, e2s, e2r, j, False).wait_send()
        slab_copy(late2_out, late2, d2s, d2r, j, False).wait_send()
        reduce_copy(red2, r2s, r2r, j, False, False).wait_send()


def body(fields, spline, measured, confidence, block_ids, live, owners):
    vmem = pl.BlockSpec(memory_space=pltpu.VMEM)
    smem = pl.BlockSpec(memory_space=pltpu.SMEM)
    dma = pltpu.SemaphoreType.DMA
    received, update = pl.pallas_call(
        kernel,
        out_shape=(
            jax.ShapeDtypeStruct((8, PEERS * CAP), F32),
            jax.ShapeDtypeStruct((1, PARAMS), F32),
        ),
        in_specs=[smem, smem, vmem, pl.BlockSpec(memory_space=pl.ANY), vmem, vmem, vmem],
        out_specs=(vmem, vmem),
        scratch_shapes=[
            pltpu.VMEM((3, 8, SLOTS, SUBSETS), BF16),
            dma,
            pltpu.VMEM((2, GRP, PACKED, HALF), BF16),
            pltpu.VMEM((2, GRP * BLOCKS, ROWS, HALF), BF16),
            pltpu.VMEM((TILES, SLOTS * BLK, 128), BF16),
            pltpu.VMEM((3, 32, 128), F32),
            pltpu.VMEM((PEERS, 128), F32),
            pltpu.VMEM((CHUNK, CHUNK + 128), BF16),
            pltpu.VMEM((BLOCKS * ROWS, PACKED), BF16),
            pltpu.VMEM((SUBSETS, 128), BF16),
            pltpu.VMEM((HIGH, SUBSETS), BF16),
            pltpu.VMEM((6 * HIGH, SUBSETS), BF16),
            pltpu.VMEM((8 * HIGH, 128), F32),
            pltpu.VMEM((24, SUBSETS), F32),
            pltpu.VMEM((8, SUBSETS), F32),
            pltpu.VMEM((48, SUBSETS), F32),
            pltpu.VMEM((128, SUBSETS), F32),
            pltpu.VMEM((GRP, 1, 128), F32),
            pltpu.VMEM((SLAB, 1, 128), F32),
            pltpu.VMEM((GRP * 16, 128), F32),
            pltpu.VMEM((GRP * 16, 128), F32),
            pltpu.VMEM((SLAB, 8, 128), F32),
            pltpu.VMEM((SLAB, 8, 128), F32),
            pltpu.VMEM((GRP * 16, 128), F32),
            pltpu.VMEM((GRP * 16, 128), F32),
            pltpu.VMEM((SLAB, 8, 128), F32),
            pltpu.VMEM((SLAB, 8, 128), F32),
            pltpu.VMEM((256, 128), F32),
            dma((2, 8, 2)), dma((2, 8, 2)),
            dma((GRP,)), dma((GRP,)), dma((SLAB,)), dma((SLAB,)),
            dma((GRP,)), dma((GRP,)), dma((SLAB,)), dma((SLAB,)),
            dma((GRP,)), dma((GRP,)), dma((SLAB,)), dma((SLAB,)),
        ],
        compiler_params=pltpu.CompilerParams(
            collective_id=0, has_side_effects=True, vmem_limit_bytes=56 * 1024 * 1024
        ),
    )(
        block_ids.T, live, fields, spline, measured,
        confidence.reshape(1, SUBSETS), owners.reshape(1, SUBSETS),
    )
    return (received, update.reshape(PARAMS))


def solution(mesh):
    placed = (
        P(None, ("slab", "grp")),
        P(None, None, None, ("slab", "grp")),
        P(None, ("slab", "grp")),
        P(("slab", "grp")),
        P(("slab", "grp"), None),
        P(("slab", "grp")),
        P(("slab", "grp"), None),
    )
    return jax.shard_map(
        body, mesh=mesh, in_specs=placed, out_specs=(P(None, ("slab", "grp")), P()), check_vma=False
    )
```

time: 783 us -> 98.7 us (0.13)
  local copies, waits for them, and re-layouts: 382 us -> 2.19 us
  blocking collectives: 145 us -> 0 us
  Pallas kernels: 0 us -> 95.7 us
  other arithmetic: 87.6 us -> 0 us
  matrix products: 84.8 us -> 0 us
  between operations: 65.5 us -> 0.65 us
  loops' own time: 14.6 us -> 0 us
    gather x19 -> x0, local copies, waits for them, and re-layouts: 331 us -> none  [the longest x13 299 us: place_slots(): run_start = jnp.searchsorted(ordered, ordered, side='left')]
    psum x1 -> x0, blocking collectives: 111 us -> none  [body(): hessian, gradient = lax.psum((hess_local, grad_local), ('slab', 'grp'))]
    pallas_call x0 -> x1, Pallas kernels: none -> 95.7 us  [body(): pl.pallas_call(kernel, out_shape=(jax.ShapeDtypeStruct((8, PEERS * CAP),...]
    dot_general x7 -> x0, matrix products: 84.8 us -> none  [the longest x4 82.2 us: interp_step(): jnp.einsum('cnkv,vkns->cns', picked, tile_set, preferred_element_type=jnp...]
    convert_element_type x12 -> x0, other arithmetic: 42 us -> none  [the longest x4 37.5 us: build_tiles(): return (product * keep_mask[None, :, :, None]).astype(jnp.bfloat16)]
    all_to_all x2 -> x0, blocking collectives: 34.3 us -> none  [the longest x1 21.1 us: body(): lax.all_to_all(lax.all_to_all(placed, 'slab', split_axis=1, concat_axis=1...]
    mul x11 -> x0, other arithmetic: 33.8 us -> none  [the longest x4 31.7 us: build_tiles(): product = product * along_x[None, None, :]]
    scatter x2 -> x0, local copies, waits for them, and re-layouts: 28.3 us -> none  [the longest x1 15.5 us: place_slots(): jnp.zeros((subset_count,), jnp.int32).at[permutation].set(rank_sorted)]
  transfers between devices with their start and end apart: 1 -> 0, of which waited for: 0 -> 0; matrix products, arithmetic and copies ran while one was open for 44% -> 0% of each run, Pallas kernels for 0% -> 0%
where the time goes in v1:
time: 98.7 us; the launch traced here: 98.5 us
  Pallas kernels  95.7 us (97%)
  local copies, waits for them, and re-layouts  2.19 us (2%)
    pallas_call x1, Pallas kernels, body(): pl.pallas_call(kernel, out_shape=(jax.ShapeDtypeStruct((8, PEERS * CAP),...  95.7 us
    unnamed x4, local copies, waits for them, and re-layouts  2.19 us

profile of v1, /device:TPU:1, one launch (start us, length us, event | category | flops | bytes accessed | tf_op | source)
XLA Modules:
  0.0 98.5 jit_solution(15093468261891177064)
XLA Ops:
  0.6 95.7 %shard_map.86 = (f32[8,8192]{1,0:T(8,128)}, f32[1,8]{1,0:T(1,128)}) custom-call(s32[4,64]{1,0:T(4,128)} %bitcast.6, s32[64]{0:T(128)} %live_ref.1, bf16[27,2048]{1,0:T(8,128)(2,1)} %fields_ref.1, bf16[3,8,4,4096]{3,2,1,0:T(4,128)(2,1)} %spline_hbm.1, f32[3,4096]{1,0:T(4,128)} %meas_ref.1, f32[1,4096]{1,0:T(1,128)} %bitcast.4, s32[1,4096]{1,0:T(1,128)} %bitcast.5), custom_call_target="tpu_custom_call" | custom-call | tf_op jit(solution)/shard_map/pallas_call | solution.py:427
  96.3 0.0 copy-start
  96.3 1.7 %copy.11 = f32[8,8192]{1,0:T(8,128)} copy(f32[8,8192]{1,0:T(8,128)} %get-tuple-element.8) | data formatting | bytes 524288
  98.0 0.0 copy-done
  98.0 0.5 copy.12
Async XLA Ops:
  96.3 1.7 %copy-start = (f32[1,8]{1,0:T(1,128)S(1)}, f32[1,8]{1,0:T(1,128)}, u32[]{:S(2)}) copy-start(f32[1,8]{1,0:T(1,128)} %get-tuple-element.5) | copy-start | bytes 100

commit v2 on v1

--- a/solution.py
+++ b/solution.py
@@ -19,7 +19,10 @@
 BLOCKS = 4
 PACKED = 112
 BLK = 512
-HALF = 256
+PIECE = 128
+PIECES = 4
+EXPRESS = 3
+STEPS = 7
 SLOTS = 4
 CAP = 16
 GRP = 16
@@ -56,18 +59,16 @@
     ids_ref, live_ref, fields_ref, spline_hbm, meas_ref, conf_ref, own_ref,
     out_ref, upd_ref,
     spline_ref, spline_sem, land, store, tiles, sp32, carry, upper_ref, unpack_ref,
-    scatter_b, scatter_m, scatter_a, early_acc, sens, resid, norm_l, norm_r,
+    scatter_b, scatter_m, scatter_a, early_acc, first_half, sens, resid, norm_l, norm_r,
     red1, red2, early_out, early1, early2_out, early2, late_out, late1, late2_out, late2, flip,
     ag_send, ag_recv, r1s, r1r, r2s, r2r, e1s, e1r, e2s, e2r, d1s, d1r, d2s, d2r,
 ):
     me_s = lax.axis_index("slab")
     me_g = lax.axis_index("grp")
-    right, left = lax.rem(me_g + 1, GRP), lax.rem(me_g + GRP - 1, GRP)
 
     barrier = pltpu.get_barrier_semaphore()
 
-    @pl.loop(1, GRP)
-    def _(j):
+    for j in (1, EXPRESS, GRP - EXPRESS, GRP - 1):
         pl.semaphore_signal(barrier, inc=1, device_id=(me_s, lax.rem(me_g + j, GRP)), device_id_type=MESH)
 
     @pl.loop(1, SLAB)
@@ -89,32 +90,34 @@
         )
         packed = part if packed is None else packed + part
     packed = packed.astype(BF16)
-    land[0, me_g] = packed[:, :HALF]
-    land[1, me_g] = packed[:, HALF:]
-
-    row, col = iota((CHUNK, CHUNK + 128), 0), iota((CHUNK, CHUNK + 128), 1)
-    upper_ref[...] = jnp.where((row < col) | (col >= CHUNK), 1.0, 0.0).astype(BF16)
-    row, col = iota((BLOCKS * ROWS, PACKED), 0), iota((BLOCKS * ROWS, PACKED), 1)
-    unpack = jnp.zeros((BLOCKS * ROWS, PACKED), F32)
-    for j in range(BLOCKS):
-        inside = (row >= ROWS * j) & (row < ROWS * j + CHANNELS)
-        unpack = jnp.where(inside & (col == row - (ROWS - CHANNELS) * j), 1.0, unpack)
-    unpack_ref[...] = unpack.astype(BF16)
-    carry[...] = jnp.zeros_like(carry)
-    early_acc[...] = jnp.zeros_like(early_acc)
-    late_out[...] = jnp.zeros_like(late_out)
-    norm_r[...] = jnp.zeros_like(norm_r)
-
-    def ring(direction, i, h, slot, target):
+    for p in range(PIECES):
+        land[p, me_g] = packed[:, p * PIECE:(p + 1) * PIECE]
+
+    def place_at(direction, distance):
+        return lax.rem(me_g + (distance if direction == 0 else GRP - distance), GRP)
+
+    def hop(direction, p, position, reach):
+        slot = place_at(1 - direction, position)
         return pltpu.make_async_remote_copy(
-            src_ref=land.at[h, slot], dst_ref=land.at[h, slot],
-            send_sem=ag_send.at[direction, i, h], recv_sem=ag_recv.at[direction, i, h],
-            device_id=(me_s, target), device_id_type=MESH,
-        )
-
-    def unpack_slot(h, slot):
-        rows = jnp.dot(unpack_ref[...], land[h, slot], preferred_element_type=F32).astype(BF16)
-        store[h, pl.ds(BLOCKS * slot, BLOCKS)] = rows.reshape(BLOCKS, ROWS, HALF)
+            src_ref=land.at[p, slot], dst_ref=land.at[p, slot],
+            send_sem=ag_send.at[direction, p, position + reach], recv_sem=ag_recv.at[direction, p, position + reach],
+            device_id=(me_s, place_at(direction, reach)), device_id_type=MESH,
+        )
+
+    def landed(direction, p, position):
+        slot = place_at(1 - direction, position)
+        pltpu.make_async_remote_copy(
+            src_ref=land.at[p, slot], dst_ref=land.at[p, slot],
+            send_sem=ag_send.at[direction, p, position], recv_sem=ag_recv.at[direction, p, position],
+            device_id=(me_s, place_at(direction, 1)), device_id_type=MESH,
+        ).wait_recv()
+
+    def unpack_slots(p, slots):
+        joined = jnp.concatenate([land[p, slot] for slot in slots], axis=1)
+        rows = jnp.dot(unpack_ref[...], joined, preferred_element_type=F32).astype(BF16)
+        for n, slot in enumerate(slots):
+            part = rows[:, n * PIECE:(n + 1) * PIECE].reshape(BLOCKS, ROWS, PIECE)
+            store[p, pl.ds(BLOCKS * slot, BLOCKS)] = part
 
     def build_tile(t):
         lanes = pl.ds(pl.multiple_of(t * 128, 128), 128)
@@ -131,7 +134,7 @@
             for z in range(8):
                 face = along_z[z:z + 1, :] * along_y
                 cells = (face[:, None, :] * along_x[None, :, :]).reshape(64, 128)
-                start = (z // 4) * 1024 + k * HALF + (z % 4) * 64
+                start = (z // 2) * 512 + k * PIECE + (z % 2) * 64
                 tiles[t, start:start + 64, :] = cells.astype(BF16)
 
     def place_chunk(j):
@@ -158,53 +161,128 @@
         )
         early_acc[...] += jnp.dot(stacked, column, preferred_element_type=F32)
 
-    pl.semaphore_wait(barrier, GRP + SLAB - 2)
-
-    @pl.loop(0, CHUNKS)
-    def _(j):
-        i, h = j // 2, j % 2
-        back, ahead = lax.rem(me_g + GRP - i, GRP), lax.rem(me_g + i, GRP)
-
-        @pl.when(i > 0)
+    pl.semaphore_wait(barrier, SLAB + 3)
+
+    def forward(direction, p, position):
+        if p % 2 == direction:
+            hop(direction, p, position, 1).start()
+        else:
+            if isinstance(position, int) and position >= 7:
+                return
+
+            @pl.when(position < 7)
+            def _():
+                hop(direction, p, position, 1).start()
+
+    first, second = (0, 1), (2, 3)
+    both = (0, 1)
+
+    for p in first:
+        for direction in both:
+            hop(direction, p, 0, EXPRESS).start()
+            hop(direction, p, 0, 1).start()
+    for p in second:
+        for direction in both:
+            hop(direction, p, 0, 1).start()
+
+    row, col = iota((CHUNK, CHUNK + 128), 0), iota((CHUNK, CHUNK + 128), 1)
+    upper_ref[...] = jnp.where((row < col) | (col >= CHUNK), 1.0, 0.0).astype(BF16)
+    row, col = iota((BLOCKS * ROWS, PACKED), 0), iota((BLOCKS * ROWS, PACKED), 1)
+    unpack = jnp.zeros((BLOCKS * ROWS, PACKED), F32)
+    for j in range(BLOCKS):
+        inside = (row >= ROWS * j) & (row < ROWS * j + CHANNELS)
+        unpack = jnp.where(inside & (col == row - (ROWS - CHANNELS) * j), 1.0, unpack)
+    unpack_ref[...] = unpack.astype(BF16)
+    carry[...] = jnp.zeros_like(carry)
+    early_acc[...] = jnp.zeros_like(early_acc)
+    norm_r[...] = jnp.zeros_like(norm_r)
+
+    spline_copy.wait()
+    for p in range(PIECES):
+        unpack_slots(p, [me_g])
+
+    def build(lo, hi):
+        @pl.loop(lo, hi)
+        def _(j):
+            build_tile(2 * j)
+            build_tile(2 * j + 1)
+            place_chunk(j)
+
+    build(0, 2)
+
+    def second_step(i):
+        for p in second:
+            for direction in both:
+                landed(direction, p, i)
+                forward(direction, p, i)
+
+    def unpack_both(p, position):
+        unpack_slots(p, [place_at(0, position), place_at(1, position)])
+
+    @pl.loop(1, STEPS)
+    def _(i):
+        second_step(i)
+
+        @pl.when(i == 1)
         def _():
-            ring(0, i - 1, h, back, right).wait_recv()
-            ring(1, i - 1, h, ahead, left).wait_recv()
-
-        @pl.when((i < 7) | (h == 0))
+            for p in first:
+                for direction in both:
+                    landed(direction, p, 1)
+                    hop(direction, p, 1, 1).start()
+
+        build(2 * i, 2 * i + 1)
+        position = i + EXPRESS - 1
+
+        for p in first:
+            for direction in both:
+                if p % 2 == direction:
+                    landed(direction, p, position)
+
+                    @pl.when(position < 8)
+                    def _():
+                        hop(direction, p, position, 1).start()
+                else:
+                    @pl.when(position < 8)
+                    def _():
+                        landed(direction, p, position)
+
+                    @pl.when(position < 7)
+                    def _():
+                        hop(direction, p, position, 1).start()
+
+        for p in second:
+            unpack_both(p, i)
+
+        build(2 * i + 1, 2 * i + 2)
+
+        @pl.when(i == 2)
         def _():
-            ring(0, i, h, back, right).start()
-
-        @pl.when((i < 7) | (h == 1))
+            for p in first:
+                for direction in both:
+                    landed(direction, p, 2)
+
+        @pl.when(i < 3)
         def _():
-            ring(1, i, h, ahead, left).start()
-
-        @pl.when(j == 0)
-        def _():
-            spline_copy.wait()
-
-        unpack_slot(h, back)
-        unpack_slot(h, ahead)
-        build_tile(2 * j)
-        build_tile(2 * j + 1)
-        place_chunk(j)
+            for p in first:
+                unpack_both(p, i)
+
+        for p in first:
+            unpack_both(p, position)
+
+    build(2 * STEPS, CHUNKS)
 
     total = early_acc[0:4 * HIGH, :] + early_acc[4 * HIGH:, :]
     for c in range(4):
         for g in range(GRP):
             early_out[16 * g + 4 * c:16 * g + 4 * c + 4, :] = total[HIGH * c + 4 * g:HIGH * c + 4 * g + 4, :]
 
-    opposite = lax.rem(me_g + 8, GRP)
-    ring(0, 7, 0, opposite, right).wait_recv()
-    ring(1, 7, 1, opposite, left).wait_recv()
-    unpack_slot(0, opposite)
-    unpack_slot(1, opposite)
-
     def group_copy(source, landing, send, recv, j, arriving):
         peer = lax.rem(me_g + j, GRP)
         origin = peer if arriving else me_g
+        flat = len(source.shape) == 2
         return pltpu.make_async_remote_copy(
-            src_ref=source.at[pl.ds(pl.multiple_of(16 * peer, 16), 16)],
-            dst_ref=landing.at[pl.ds(pl.multiple_of(16 * origin, 16), 16)],
+            src_ref=source.at[pl.ds(pl.multiple_of(16 * peer, 16), 16)] if flat else source.at[peer],
+            dst_ref=landing.at[pl.ds(pl.multiple_of(16 * origin, 16), 16)] if flat else landing.at[origin],
             send_sem=send.at[peer], recv_sem=recv.at[origin],
             device_id=(me_s, peer), device_id_type=MESH,
         )
@@ -229,26 +307,36 @@
             device_id=(me_s, peer) if along_group else (peer, me_g), device_id_type=MESH,
         )
 
-    @pl.loop(1, GRP)
-    def _(j):
-        group_copy(early_out, early1, e1s, e1r, j, False).start()
-
-    mine = pl.ds(pl.multiple_of(16 * me_g, 16), 16)
-    early1[mine, :] = early_out[mine, :]
-
-    @pl.loop(0, TILES)
-    def _(t):
-        lanes = pl.ds(pl.multiple_of(t * 128, 128), 128)
+    def interpolate(t, half):
         rows = []
         for part in range(2):
             rows.append(
                 jnp.concatenate(
-                    [store[h, ids_ref[k, 2 * t + part]] for h in range(2) for k in range(SLOTS)], axis=1
+                    [store[p, ids_ref[k, 2 * t + part]] for p in (2 * half, 2 * half + 1) for k in range(SLOTS)], axis=1
                 )
             )
-        both = jnp.dot(jnp.concatenate(rows, axis=0), tiles[t], preferred_element_type=F32)
-        lane = iota((ROWS, 128), 1)
-        modelled = jnp.where(lane < 64, both[:ROWS], both[ROWS:])
+        both = jnp.dot(
+            jnp.concatenate(rows, axis=0), tiles[t, 1024 * half:1024 * half + 1024], preferred_element_type=F32
+        )
+        return jnp.where(iota((ROWS, 128), 1) < 64, both[:ROWS], both[ROWS:])
+
+    def interpolate_first(lo, hi):
+        @pl.loop(lo, hi, unroll=2)
+        def _(t):
+            first_half[:, pl.ds(pl.multiple_of(t * 128, 128), 128)] = interpolate(t, 0)
+
+    interpolate_first(0, 8)
+    second_step(STEPS)
+    interpolate_first(8, TILES)
+    for p in second:
+        unpack_both(p, STEPS)
+        landed(p % 2, p, STEPS + 1)
+        unpack_slots(p, [place_at(0, STEPS + 1)])
+
+    @pl.loop(0, TILES, unroll=2)
+    def _(t):
+        lanes = pl.ds(pl.multiple_of(t * 128, 128), 128)
+        modelled = first_half[:, lanes] + interpolate(t, 1)
         weight = conf_ref[:, lanes]
         residual = meas_ref[:, lanes] - modelled[24:27]
         sens[:, lanes] = modelled[:24]
@@ -281,23 +369,20 @@
     def _(j):
         reduce_copy(red1, r1s, r1r, j, False, True).start()
 
-    @pl.loop(1, GRP)
-    def _(j):
-        group_copy(early_out, early1, e1s, e1r, j, True).wait_recv()
-
     def turn(landing, outgoing, comps):
         for c in range(comps):
             for upper_part in range(4):
                 for side in range(2):
-                    block = landing[pl.ds(128 * side + 4 * c + upper_part, 8, stride=16), :]
+                    if len(landing.shape) == 2:
+                        block = landing[pl.ds(128 * side + 4 * c + upper_part, 8, stride=16), :]
+                    else:
+                        block = landing[8 * side:8 * side + 8, c, upper_part, :]
                     start = 64 * upper_part + 8 * (4 * side + c)
                     flip[start:start + 8, :] = swap_chunks(block)
         for upper_part in range(4):
             for lower_part in range(8):
                 outgoing[8 * upper_part + lower_part] = flip[pl.ds(64 * upper_part + lower_part, 8, stride=8), :]
 
-    turn(early1, early2_out, 4)
-
     @pl.loop(1, GRP)
     def _(j):
         reduce_copy(red1, r1s, r1r, j, True, True).wait_recv()
@@ -308,11 +393,12 @@
     def _(j):
         reduce_copy(red2, r2s, r2r, j, False, False).start()
 
-    @pl.loop(1, SLAB)
-    def _(j):
-        slab_copy(early2_out, early2, e2s, e2r, j, False).start()
-
-    early2[me_s] = early2_out[me_s]
+    @pl.loop(1, GRP)
+    def _(j):
+        group_copy(early_out, early1, e1s, e1r, j, False).start()
+
+    mine = pl.ds(pl.multiple_of(16 * me_g, 16), 16)
+    early1[mine, :] = early_out[mine, :]
 
     @pl.loop(1, SLAB)
     def _(j):
@@ -344,13 +430,25 @@
     placed = placed[:3 * HIGH] + placed[3 * HIGH:]
     for c in range(COMPS):
         for g in range(GRP):
-            late_out[16 * g + 4 * c:16 * g + 4 * c + 4, :] = placed[HIGH * c + 4 * g:HIGH * c + 4 * g + 4, :]
+            late_out[g, c] = placed[HIGH * c + 4 * g:HIGH * c + 4 * g + 4, :]
 
     @pl.loop(1, GRP)
     def _(j):
         group_copy(late_out, late1, d1s, d1r, j, False).start()
 
-    late1[mine, :] = late_out[mine, :]
+    late1[me_g] = late_out[me_g]
+
+    @pl.loop(1, GRP)
+    def _(j):
+        group_copy(early_out, early1, e1s, e1r, j, True).wait_recv()
+
+    turn(early1, early2_out, 4)
+
+    @pl.loop(1, SLAB)
+    def _(j):
+        slab_copy(early2_out, early2, e2s, e2r, j, False).start()
+
+    early2[me_s] = early2_out[me_s]
 
     @pl.loop(1, GRP)
     def _(j):
@@ -394,18 +492,11 @@
                 start = 256 * (first + n) + 128 * side
                 out_ref[:, start:start + 128] = flip[pl.ds(n, 8, stride=8), :]
 
-    @pl.loop(0, CHUNKS)
-    def _(j):
-        i, h = j // 2, j % 2
-        back, ahead = lax.rem(me_g + GRP - i, GRP), lax.rem(me_g + i, GRP)
-
-        @pl.when((i < 7) | (h == 0))
-        def _():
-            ring(0, i, h, back, right).wait_send()
-
-        @pl.when((i < 7) | (h == 1))
-        def _():
-            ring(1, i, h, ahead, left).wait_send()
+    for p in range(PIECES):
+        for direction in both:
+            @pl.loop(1, 9 if p % 2 == direction else 8)
+            def _(position):
+                hop(direction, p, position - 1, 1).wait_send()
 
     @pl.loop(1, GRP)
     def _(j):
@@ -435,8 +526,8 @@
         scratch_shapes=[
             pltpu.VMEM((3, 8, SLOTS, SUBSETS), BF16),
             dma,
-            pltpu.VMEM((2, GRP, PACKED, HALF), BF16),
-            pltpu.VMEM((2, GRP * BLOCKS, ROWS, HALF), BF16),
+            pltpu.VMEM((PIECES, GRP, PACKED, PIECE), BF16),
+            pltpu.VMEM((PIECES, GRP * BLOCKS, ROWS, PIECE), BF16),
             pltpu.VMEM((TILES, SLOTS * BLK, 128), BF16),
             pltpu.VMEM((3, 32, 128), F32),
             pltpu.VMEM((PEERS, 128), F32),
@@ -446,6 +537,7 @@
             pltpu.VMEM((HIGH, SUBSETS), BF16),
             pltpu.VMEM((6 * HIGH, SUBSETS), BF16),
             pltpu.VMEM((8 * HIGH, 128), F32),
+            pltpu.VMEM((ROWS, SUBSETS), F32),
             pltpu.VMEM((24, SUBSETS), F32),
             pltpu.VMEM((8, SUBSETS), F32),
             pltpu.VMEM((48, SUBSETS), F32),
@@ -456,12 +548,12 @@
             pltpu.VMEM((GRP * 16, 128), F32),
             pltpu.VMEM((SLAB, 8, 128), F32),
             pltpu.VMEM((SLAB, 8, 128), F32),
-            pltpu.VMEM((GRP * 16, 128), F32),
-            pltpu.VMEM((GRP * 16, 128), F32),
+            pltpu.VMEM((GRP, COMPS, 4, 128), F32),
+            pltpu.VMEM((GRP, COMPS, 4, 128), F32),
             pltpu.VMEM((SLAB, 8, 128), F32),
             pltpu.VMEM((SLAB, 8, 128), F32),
             pltpu.VMEM((256, 128), F32),
-            dma((2, 8, 2)), dma((2, 8, 2)),
+            dma((2, PIECES, 9)), dma((2, PIECES, 9)),
             dma((GRP,)), dma((GRP,)), dma((SLAB,)), dma((SLAB,)),
             dma((GRP,)), dma((GRP,)), dma((SLAB,)), dma((SLAB,)),
             dma((GRP,)), dma((GRP,)), dma((SLAB,)), dma((SLAB,)),

time: 98.7 us -> 94 us (0.952)
  Pallas kernels: 95.7 us -> 91 us
    pallas_call x1, Pallas kernels: 95.7 us -> 91 us  [body(): pl.pallas_call(kernel, out_shape=(jax.ShapeDtypeStruct((8, PEERS * CAP),...]
where the time goes in v2:
time: 94 us; the launch traced here: 93.8 us
  Pallas kernels  91 us (97%)
  local copies, waits for them, and re-layouts  2.19 us (2%)
    pallas_call x1, Pallas kernels, body(): pl.pallas_call(kernel, out_shape=(jax.ShapeDtypeStruct((8, PEERS * CAP),...  91 us
    unnamed x4, local copies, waits for them, and re-layouts  2.19 us

profile of v2, /device:TPU:1, one launch (start us, length us, event | category | flops | bytes accessed | tf_op | source)
XLA Modules:
  0.0 93.8 jit_solution(9813752540834583935)
XLA Ops:
  0.6 91.0 %shard_map.86 = (f32[8,8192]{1,0:T(8,128)}, f32[1,8]{1,0:T(1,128)}) custom-call(s32[4,64]{1,0:T(4,128)} %bitcast.6, s32[64]{0:T(128)} %live_ref.1, bf16[27,2048]{1,0:T(8,128)(2,1)} %fields_ref.1, bf16[3,8,4,4096]{3,2,1,0:T(4,128)(2,1)} %spline_hbm.1, f32[3,4096]{1,0:T(4,128)} %meas_ref.1, f32[1,4096]{1,0:T(1,128)} %bitcast.4, s32[1,4096]{1,0:T(1,128)} %bitcast.5), custom_call_target="tpu_custom_call" | custom-call | tf_op jit(solution)/shard_map/pallas_call | solution.py:518
  91.7 0.0 copy-start
  91.7 1.7 %copy.11 = f32[8,8192]{1,0:T(8,128)} copy(f32[8,8192]{1,0:T(8,128)} %get-tuple-element.8) | data formatting | bytes 524288
  93.3 0.0 copy-done
  93.3 0.5 copy.12
Async XLA Ops:
  91.7 1.7 %copy-start = (f32[1,8]{1,0:T(1,128)S(1)}, f32[1,8]{1,0:T(1,128)}, u32[]{:S(2)}) copy-start(f32[1,8]{1,0:T(1,128)} %get-tuple-element.5) | copy-start | bytes 100

commit v3 on v2

--- a/solution.py
+++ b/solution.py
@@ -21,8 +21,7 @@
 BLK = 512
 PIECE = 128
 PIECES = 4
-EXPRESS = 3
-STEPS = 7
+STEPS = 6
 SLOTS = 4
 CAP = 16
 GRP = 16
@@ -59,7 +58,7 @@
     ids_ref, live_ref, fields_ref, spline_hbm, meas_ref, conf_ref, own_ref,
     out_ref, upd_ref,
     spline_ref, spline_sem, land, store, tiles, sp32, carry, upper_ref, unpack_ref,
-    scatter_b, scatter_m, scatter_a, early_acc, first_half, sens, resid, norm_l, norm_r,
+    scatter_b, scatter_m, early_acc, first_half, sens, resid, norm_l, norm_r,
     red1, red2, early_out, early1, early2_out, early2, late_out, late1, late2_out, late2, flip,
     ag_send, ag_recv, r1s, r1r, r2s, r2r, e1s, e1r, e2s, e2r, d1s, d1r, d2s, d2r,
 ):
@@ -68,7 +67,7 @@
 
     barrier = pltpu.get_barrier_semaphore()
 
-    for j in (1, EXPRESS, GRP - EXPRESS, GRP - 1):
+    for j in (1, 2, GRP - 2, GRP - 1):
         pl.semaphore_signal(barrier, inc=1, device_id=(me_s, lax.rem(me_g + j, GRP)), device_id_type=MESH)
 
     @pl.loop(1, SLAB)
@@ -151,37 +150,31 @@
         high = (owner & 15) * 4 + (owner >> 7)
         column = jnp.where(iota((128, CHUNK), 0) == low, 1.0, 0.0).T.astype(BF16)
         scatter_b[lanes, :] = column
-        mask = jnp.where(iota((HIGH, CHUNK), 0) == high, 1.0, 0.0)
-        scatter_m[:, lanes] = mask.astype(BF16)
+        mask = jnp.where(iota((HIGH, CHUNK), 0) == high, 1.0, 0.0).astype(BF16)
+        scatter_m[:, lanes] = mask
         pieces = []
         for value in [meas_ref[c:c + 1, lanes] for c in range(COMPS)] + [conf_ref[:, lanes]]:
             pieces.append(split_two(value))
         stacked = jnp.concatenate(
-            [(mask * pieces[c][part]).astype(BF16) for part in range(2) for c in range(4)], axis=0
+            [mask * pieces[c][part].astype(BF16) for part in range(2) for c in range(4)], axis=0
         )
         early_acc[...] += jnp.dot(stacked, column, preferred_element_type=F32)
 
     pl.semaphore_wait(barrier, SLAB + 3)
 
-    def forward(direction, p, position):
-        if p % 2 == direction:
-            hop(direction, p, position, 1).start()
-        else:
-            if isinstance(position, int) and position >= 7:
-                return
-
-            @pl.when(position < 7)
+    both = (0, 1)
+
+    def send_step(p, step, position):
+        for direction in both:
+            @pl.when((step < STEPS - 1) | (p % 2 == direction))
+            def _():
+                hop(direction, p, position, 1 + (step % 3) // 2).start()
+
+            @pl.when(step % 3 == 2)
             def _():
                 hop(direction, p, position, 1).start()
 
-    first, second = (0, 1), (2, 3)
-    both = (0, 1)
-
-    for p in first:
-        for direction in both:
-            hop(direction, p, 0, EXPRESS).start()
-            hop(direction, p, 0, 1).start()
-    for p in second:
+    for p in range(PIECES):
         for direction in both:
             hop(direction, p, 0, 1).start()
 
@@ -197,10 +190,6 @@
     early_acc[...] = jnp.zeros_like(early_acc)
     norm_r[...] = jnp.zeros_like(norm_r)
 
-    spline_copy.wait()
-    for p in range(PIECES):
-        unpack_slots(p, [me_g])
-
     def build(lo, hi):
         @pl.loop(lo, hi)
         def _(j):
@@ -208,68 +197,35 @@
             build_tile(2 * j + 1)
             place_chunk(j)
 
-    build(0, 2)
-
-    def second_step(i):
-        for p in second:
-            for direction in both:
-                landed(direction, p, i)
-                forward(direction, p, i)
-
     def unpack_both(p, position):
         unpack_slots(p, [place_at(0, position), place_at(1, position)])
 
+    spline_copy.wait()
+    for p in range(PIECES):
+        unpack_slots(p, [me_g])
+    build(0, 2)
+
     @pl.loop(1, STEPS)
-    def _(i):
-        second_step(i)
-
-        @pl.when(i == 1)
-        def _():
-            for p in first:
+    def _(step):
+        position = step + step // 3
+        for group in range(2):
+            pieces = (2 * group, 2 * group + 1)
+            for p in pieces:
                 for direction in both:
-                    landed(direction, p, 1)
-                    hop(direction, p, 1, 1).start()
-
-        build(2 * i, 2 * i + 1)
-        position = i + EXPRESS - 1
-
-        for p in first:
-            for direction in both:
-                if p % 2 == direction:
                     landed(direction, p, position)
-
-                    @pl.when(position < 8)
-                    def _():
-                        hop(direction, p, position, 1).start()
-                else:
-                    @pl.when(position < 8)
-                    def _():
-                        landed(direction, p, position)
-
-                    @pl.when(position < 7)
-                    def _():
-                        hop(direction, p, position, 1).start()
-
-        for p in second:
-            unpack_both(p, i)
-
-        build(2 * i + 1, 2 * i + 2)
-
-        @pl.when(i == 2)
-        def _():
-            for p in first:
-                for direction in both:
-                    landed(direction, p, 2)
-
-        @pl.when(i < 3)
-        def _():
-            for p in first:
-                unpack_both(p, i)
-
-        for p in first:
-            unpack_both(p, position)
-
-    build(2 * STEPS, CHUNKS)
+                send_step(p, step, position)
+            for p in pieces:
+                unpack_both(p, position)
+
+            @pl.when(step == 3)
+            def _():
+                for p in pieces:
+                    for direction in both:
+                        landed(direction, p, 3)
+                    unpack_both(p, 3)
+
+            turn_index = 2 * (step - 1) + group
+            build(2 + (turn_index * 7) // 5, 2 + ((turn_index + 1) * 7) // 5)
 
     total = early_acc[0:4 * HIGH, :] + early_acc[4 * HIGH:, :]
     for c in range(4):
@@ -291,7 +247,8 @@
         peer = lax.rem(me_s + j, SLAB)
         origin = peer if arriving else me_s
         return pltpu.make_async_remote_copy(
-            src_ref=source.at[peer], dst_ref=landing.at[origin],
+            src_ref=source.at[pl.ds(pl.multiple_of(8 * peer, 8), 8)],
+            dst_ref=landing.at[pl.ds(pl.multiple_of(8 * origin, 8), 8)],
             send_sem=send.at[peer], recv_sem=recv.at[origin],
             device_id=(peer, me_g), device_id_type=MESH,
         )
@@ -320,18 +277,22 @@
         )
         return jnp.where(iota((ROWS, 128), 1) < 64, both[:ROWS], both[ROWS:])
 
-    def interpolate_first(lo, hi):
-        @pl.loop(lo, hi, unroll=2)
-        def _(t):
-            first_half[:, pl.ds(pl.multiple_of(t * 128, 128), 128)] = interpolate(t, 0)
-
-    interpolate_first(0, 8)
-    second_step(STEPS)
-    interpolate_first(8, TILES)
-    for p in second:
-        unpack_both(p, STEPS)
-        landed(p % 2, p, STEPS + 1)
-        unpack_slots(p, [place_at(0, STEPS + 1)])
+    def last_pieces(pieces):
+        for p in pieces:
+            for direction in both:
+                landed(direction, p, 7)
+            unpack_both(p, 7)
+        for p in pieces:
+            landed(p % 2, p, 8)
+            unpack_slots(p, [place_at(0, 8)])
+
+    last_pieces((0, 1))
+
+    @pl.loop(0, TILES, unroll=2)
+    def _(t):
+        first_half[:, pl.ds(pl.multiple_of(t * 128, 128), 128)] = interpolate(t, 0)
+
+    last_pieces((2, 3))
 
     @pl.loop(0, TILES, unroll=2)
     def _(t):
@@ -381,7 +342,8 @@
                     flip[start:start + 8, :] = swap_chunks(block)
         for upper_part in range(4):
             for lower_part in range(8):
-                outgoing[8 * upper_part + lower_part] = flip[pl.ds(64 * upper_part + lower_part, 8, stride=8), :]
+                start = 64 * upper_part + 8 * lower_part
+                outgoing[start:start + 8, :] = flip[pl.ds(64 * upper_part + lower_part, 8, stride=8), :]
 
     @pl.loop(1, GRP)
     def _(j):
@@ -417,16 +379,18 @@
     flat = jnp.sum(jnp.where(lane == sub, update, 0.0), axis=0, keepdims=True)
     upd_ref[...] = flat[:, :PARAMS]
 
+    placed = jnp.zeros((6 * HIGH, 128), F32)
     for q in range(8):
         lanes = slice(512 * q, 512 * (q + 1))
-        mask = scatter_m[:, lanes].astype(F32)
+        mask = scatter_m[:, lanes]
+        pieces = []
         for c in range(COMPS):
             predicted = jnp.sum(sens[8 * c:8 * c + 8, lanes] * update, axis=0, keepdims=True)
-            remaining = split_two(resid[c:c + 1, lanes] - predicted)
-            for part in range(2):
-                start = HIGH * (3 * part + c)
-                scatter_a[start:start + HIGH, lanes] = (mask * remaining[part]).astype(BF16)
-    placed = jnp.dot(scatter_a[...], scatter_b[...], preferred_element_type=F32)
+            pieces.append(split_two(resid[c:c + 1, lanes] - predicted))
+        stacked = jnp.concatenate(
+            [mask * pieces[c][part].astype(BF16) for part in range(2) for c in range(COMPS)], axis=0
+        )
+        placed = placed + jnp.dot(stacked, scatter_b[lanes, :], preferred_element_type=F32)
     placed = placed[:3 * HIGH] + placed[3 * HIGH:]
     for c in range(COMPS):
         for g in range(GRP):
@@ -448,7 +412,8 @@
     def _(j):
         slab_copy(early2_out, early2, e2s, e2r, j, False).start()
 
-    early2[me_s] = early2_out[me_s]
+    own_rows = pl.ds(pl.multiple_of(8 * me_s, 8), 8)
+    early2[own_rows, :] = early2_out[own_rows, :]
 
     @pl.loop(1, GRP)
     def _(j):
@@ -460,7 +425,7 @@
     def _(j):
         slab_copy(late2_out, late2, d2s, d2r, j, False).start()
 
-    late2[me_s] = late2_out[me_s]
+    late2[own_rows, :] = late2_out[own_rows, :]
 
     @pl.loop(1, SLAB)
     def _(j):
@@ -473,7 +438,7 @@
     for first in range(0, SLAB, 8):
         for side in range(2):
             def rows_of(ref, c):
-                return jnp.concatenate([ref[first + n, 4 * side + c:4 * side + c + 1, :] for n in range(8)], axis=0)
+                return ref[pl.ds(8 * first + 4 * side + c, 8, stride=8), :]
 
             confidence = rows_of(early2, 3)
             squares = jnp.zeros_like(confidence)
@@ -535,7 +500,6 @@
             pltpu.VMEM((BLOCKS * ROWS, PACKED), BF16),
             pltpu.VMEM((SUBSETS, 128), BF16),
             pltpu.VMEM((HIGH, SUBSETS), BF16),
-            pltpu.VMEM((6 * HIGH, SUBSETS), BF16),
             pltpu.VMEM((8 * HIGH, 128), F32),
             pltpu.VMEM((ROWS, SUBSETS), F32),
             pltpu.VMEM((24, SUBSETS), F32),
@@ -546,12 +510,12 @@
             pltpu.VMEM((SLAB, 1, 128), F32),
             pltpu.VMEM((GRP * 16, 128), F32),
             pltpu.VMEM((GRP * 16, 128), F32),
-            pltpu.VMEM((SLAB, 8, 128), F32),
-            pltpu.VMEM((SLAB, 8, 128), F32),
+            pltpu.VMEM((SLAB * 8, 128), F32),
+            pltpu.VMEM((SLAB * 8, 128), F32),
             pltpu.VMEM((GRP, COMPS, 4, 128), F32),
             pltpu.VMEM((GRP, COMPS, 4, 128), F32),
-            pltpu.VMEM((SLAB, 8, 128), F32),
-            pltpu.VMEM((SLAB, 8, 128), F32),
+            pltpu.VMEM((SLAB * 8, 128), F32),
+            pltpu.VMEM((SLAB * 8, 128), F32),
             pltpu.VMEM((256, 128), F32),
             dma((2, PIECES, 9)), dma((2, PIECES, 9)),
             dma((GRP,)), dma((GRP,)), dma((SLAB,)), dma((SLAB,)),

time: 94 us -> 88.9 us (0.946)
  Pallas kernels: 91 us -> 85.9 us
    pallas_call x1, Pallas kernels: 91 us -> 85.9 us  [body(): pl.pallas_call(kernel, out_shape=(jax.ShapeDtypeStruct((8, PEERS * CAP),...]
where the time goes in v3:
time: 88.9 us; the launch traced here: 88.7 us
  Pallas kernels  85.9 us (97%)
  local copies, waits for them, and re-layouts  2.19 us (2%)
    pallas_call x1, Pallas kernels, body(): pl.pallas_call(kernel, out_shape=(jax.ShapeDtypeStruct((8, PEERS * CAP),...  85.9 us
    unnamed x4, local copies, waits for them, and re-layouts  2.19 us

profile of v3, /device:TPU:1, one launch (start us, length us, event | category | flops | bytes accessed | tf_op | source)
XLA Modules:
  0.0 88.7 jit_solution(13269508756657504908)
XLA Ops:
  0.6 85.9 %shard_map.86 = (f32[8,8192]{1,0:T(8,128)}, f32[1,8]{1,0:T(1,128)}) custom-call(s32[4,64]{1,0:T(4,128)} %bitcast.6, s32[64]{0:T(128)} %live_ref.1, bf16[27,2048]{1,0:T(8,128)(2,1)} %fields_ref.1, bf16[3,8,4,4096]{3,2,1,0:T(4,128)(2,1)} %spline_hbm.1, f32[3,4096]{1,0:T(4,128)} %meas_ref.1, f32[1,4096]{1,0:T(1,128)} %bitcast.4, s32[1,4096]{1,0:T(1,128)} %bitcast.5), custom_call_target="tpu_custom_call" | custom-call | tf_op jit(solution)/shard_map/pallas_call | solution.py:483
  86.5 0.0 copy-start
  86.5 1.7 %copy.11 = f32[8,8192]{1,0:T(8,128)} copy(f32[8,8192]{1,0:T(8,128)} %get-tuple-element.8) | data formatting | bytes 524288
  88.2 0.0 copy-done
  88.2 0.5 copy.12
Async XLA Ops:
  86.5 1.7 %copy-start = (f32[1,8]{1,0:T(1,128)S(1)}, f32[1,8]{1,0:T(1,128)}, u32[]{:S(2)}) copy-start(f32[1,8]{1,0:T(1,128)} %get-tuple-element.5) | copy-start | bytes 100

commit v4 on v3

--- a/solution.py
+++ b/solution.py
@@ -27,7 +27,6 @@
 GRP = 16
 SLAB = 32
 SUBSETS = 4096
-TILES = 32
 CHUNK = 256
 CHUNKS = 16
 PEERS = 512
@@ -58,7 +57,7 @@
     ids_ref, live_ref, fields_ref, spline_hbm, meas_ref, conf_ref, own_ref,
     out_ref, upd_ref,
     spline_ref, spline_sem, land, store, tiles, sp32, carry, upper_ref, unpack_ref,
-    scatter_b, scatter_m, early_acc, first_half, sens, resid, norm_l, norm_r,
+    scatter_b, scatter_m, early_acc, first_half, sens, resid, gram_ref,
     red1, red2, early_out, early1, early2_out, early2, late_out, late1, late2_out, late2, flip,
     ag_send, ag_recv, r1s, r1r, r2s, r2r, e1s, e1r, e2s, e2r, d1s, d1r, d2s, d2r,
 ):
@@ -118,7 +117,8 @@
             part = rows[:, n * PIECE:(n + 1) * PIECE].reshape(BLOCKS, ROWS, PIECE)
             store[p, pl.ds(BLOCKS * slot, BLOCKS)] = part
 
-    def build_tile(t):
+    def build_tile(j, side):
+        t = 2 * j + side
         lanes = pl.ds(pl.multiple_of(t * 128, 128), 128)
         for axis in range(3):
             part = spline_ref[axis, :, :, lanes].astype(F32)
@@ -134,7 +134,7 @@
                 face = along_z[z:z + 1, :] * along_y
                 cells = (face[:, None, :] * along_x[None, :, :]).reshape(64, 128)
                 start = (z // 2) * 512 + k * PIECE + (z % 2) * 64
-                tiles[t, start:start + 64, :] = cells.astype(BF16)
+                tiles[j, start:start + 64, 128 * side:128 * side + 128] = cells.astype(BF16)
 
     def place_chunk(j):
         lanes = pl.ds(pl.multiple_of(j * CHUNK, CHUNK), CHUNK)
@@ -188,13 +188,12 @@
     unpack_ref[...] = unpack.astype(BF16)
     carry[...] = jnp.zeros_like(carry)
     early_acc[...] = jnp.zeros_like(early_acc)
-    norm_r[...] = jnp.zeros_like(norm_r)
 
     def build(lo, hi):
         @pl.loop(lo, hi)
         def _(j):
-            build_tile(2 * j)
-            build_tile(2 * j + 1)
+            build_tile(j, 0)
+            build_tile(j, 1)
             place_chunk(j)
 
     def unpack_both(p, position):
@@ -232,6 +231,16 @@
         for g in range(GRP):
             early_out[16 * g + 4 * c:16 * g + 4 * c + 4, :] = total[HIGH * c + 4 * g:HIGH * c + 4 * g + 4, :]
 
+    def far_group(n):
+        return GRP // 2 + (n // 2) * (2 * (n % 2) - 1)
+
+    def far_slab(n):
+        def order(k):
+            return (18 - k - k * (k - 1) // 2) % 4
+
+        x, y = (me_s // 8 + order(n // 8)) % 4, ((me_s // 2) % 4 + order((n // 2) % 4)) % 4
+        return x * 8 + y * 2 + (me_s + 1 + n) % 2
+
     def group_copy(source, landing, send, recv, j, arriving):
         peer = lax.rem(me_g + j, GRP)
         origin = peer if arriving else me_g
@@ -264,18 +273,23 @@
             device_id=(me_s, peer) if along_group else (peer, me_g), device_id_type=MESH,
         )
 
-    def interpolate(t, half):
+    def interpolate(j, half):
         rows = []
-        for part in range(2):
+        for n in range(4):
             rows.append(
                 jnp.concatenate(
-                    [store[p, ids_ref[k, 2 * t + part]] for p in (2 * half, 2 * half + 1) for k in range(SLOTS)], axis=1
+                    [store[p, ids_ref[k, 4 * j + n]] for p in (2 * half, 2 * half + 1) for k in range(SLOTS)], axis=1
                 )
             )
-        both = jnp.dot(
-            jnp.concatenate(rows, axis=0), tiles[t, 1024 * half:1024 * half + 1024], preferred_element_type=F32
-        )
-        return jnp.where(iota((ROWS, 128), 1) < 64, both[:ROWS], both[ROWS:])
+        crossed = jnp.dot(
+            jnp.concatenate(rows, axis=0), tiles[j, 1024 * half:1024 * half + 1024], preferred_element_type=F32
+        )
+        left_block = iota((ROWS, 128), 1) < 64
+        sides = []
+        for side in range(2):
+            part = crossed[2 * ROWS * side:2 * ROWS * side + 2 * ROWS, 128 * side:128 * side + 128]
+            sides.append(jnp.where(left_block, part[:ROWS], part[ROWS:]))
+        return jnp.concatenate(sides, axis=1)
 
     def last_pieces(pieces):
         for p in pieces:
@@ -288,34 +302,38 @@
 
     last_pieces((0, 1))
 
-    @pl.loop(0, TILES, unroll=2)
-    def _(t):
-        first_half[:, pl.ds(pl.multiple_of(t * 128, 128), 128)] = interpolate(t, 0)
+    @pl.loop(0, CHUNKS, unroll=2)
+    def _(j):
+        first_half[:, pl.ds(pl.multiple_of(j * CHUNK, CHUNK), CHUNK)] = interpolate(j, 0)
 
     last_pieces((2, 3))
 
-    @pl.loop(0, TILES, unroll=2)
-    def _(t):
-        lanes = pl.ds(pl.multiple_of(t * 128, 128), 128)
-        modelled = first_half[:, lanes] + interpolate(t, 1)
+    gram_ref[...] = jnp.zeros_like(gram_ref)
+
+    @pl.loop(0, CHUNKS, unroll=2)
+    def _(j):
+        lanes = pl.ds(pl.multiple_of(j * CHUNK, CHUNK), CHUNK)
+        modelled = first_half[:, lanes] + interpolate(j, 1)
         weight = conf_ref[:, lanes]
         residual = meas_ref[:, lanes] - modelled[24:27]
         sens[:, lanes] = modelled[:24]
         resid[0:3, lanes] = residual
-        upper, lower = split_two(modelled[:24])
-        norm_l[0:24, lanes] = upper
-        norm_l[24:48, lanes] = lower
-        weighted = [split_two(modelled[8 * c:8 * c + 8] * weight) for c in range(COMPS)]
-        right_side = split_two(residual * weight)
-        for part in range(2):
-            for c in range(COMPS):
-                start = 64 * part + 16 * c
-                norm_r[start:start + 8, lanes] = weighted[c][part]
-                norm_r[start + 8:start + 9, lanes] = right_side[part][c:c + 1]
-
-    gram = lax.dot_general(
-        norm_l[...].astype(BF16), norm_r[...].astype(BF16), (((1,), (1,)), ((), ())), preferred_element_type=F32
-    )
+        left_side = jnp.concatenate(split_two(modelled[:24]), axis=0).astype(BF16)
+        zeros = jnp.zeros((7, CHUNK), F32)
+        weighted = jnp.concatenate(
+            [
+                piece
+                for c in range(COMPS)
+                for piece in (modelled[8 * c:8 * c + 8] * weight, residual[c:c + 1] * weight, zeros)
+            ] + [jnp.zeros((16, CHUNK), F32)],
+            axis=0,
+        )
+        right_side = jnp.concatenate(split_two(weighted), axis=0).astype(BF16)
+        gram_ref[...] += lax.dot_general(
+            left_side, right_side, (((1,), (1,)), ((), ())), preferred_element_type=F32
+        )
+
+    gram = gram_ref[...]
     gram = gram[:24] + gram[24:]
     gram = gram + pltpu.roll(gram, 64, 1)
     normal = gram[:8] + pltpu.roll(gram[8:16], 112, 1) + pltpu.roll(gram[16:24], 96, 1)
@@ -328,7 +346,7 @@
 
     @pl.loop(1, GRP)
     def _(j):
-        reduce_copy(red1, r1s, r1r, j, False, True).start()
+        reduce_copy(red1, r1s, r1r, far_group(j), False, True).start()
 
     def turn(landing, outgoing, comps):
         for c in range(comps):
@@ -351,13 +369,13 @@
 
     red2[me_s] = jnp.sum(red1[...], axis=0)
 
-    @pl.loop(1, SLAB)
-    def _(j):
-        reduce_copy(red2, r2s, r2r, j, False, False).start()
-
-    @pl.loop(1, GRP)
-    def _(j):
-        group_copy(early_out, early1, e1s, e1r, j, False).start()
+    @pl.loop(0, SLAB - 1)
+    def _(j):
+        reduce_copy(red2, r2s, r2r, far_slab(j) + SLAB - me_s, False, False).start()
+
+    @pl.loop(1, GRP)
+    def _(j):
+        group_copy(early_out, early1, e1s, e1r, far_group(j), False).start()
 
     mine = pl.ds(pl.multiple_of(16 * me_g, 16), 16)
     early1[mine, :] = early_out[mine, :]
@@ -398,7 +416,7 @@
 
     @pl.loop(1, GRP)
     def _(j):
-        group_copy(late_out, late1, d1s, d1r, j, False).start()
+        group_copy(late_out, late1, d1s, d1r, far_group(j), False).start()
 
     late1[me_g] = late_out[me_g]
 
@@ -408,9 +426,9 @@
 
     turn(early1, early2_out, 4)
 
-    @pl.loop(1, SLAB)
-    def _(j):
-        slab_copy(early2_out, early2, e2s, e2r, j, False).start()
+    @pl.loop(0, SLAB - 1)
+    def _(j):
+        slab_copy(early2_out, early2, e2s, e2r, far_slab(j) + SLAB - me_s, False).start()
 
     own_rows = pl.ds(pl.multiple_of(8 * me_s, 8), 8)
     early2[own_rows, :] = early2_out[own_rows, :]
@@ -421,9 +439,9 @@
 
     turn(late1, late2_out, 3)
 
-    @pl.loop(1, SLAB)
-    def _(j):
-        slab_copy(late2_out, late2, d2s, d2r, j, False).start()
+    @pl.loop(0, SLAB - 1)
+    def _(j):
+        slab_copy(late2_out, late2, d2s, d2r, far_slab(j) + SLAB - me_s, False).start()
 
     late2[own_rows, :] = late2_out[own_rows, :]
 
@@ -493,7 +511,7 @@
             dma,
             pltpu.VMEM((PIECES, GRP, PACKED, PIECE), BF16),
             pltpu.VMEM((PIECES, GRP * BLOCKS, ROWS, PIECE), BF16),
-            pltpu.VMEM((TILES, SLOTS * BLK, 128), BF16),
+            pltpu.VMEM((CHUNKS, SLOTS * BLK, CHUNK), BF16),
             pltpu.VMEM((3, 32, 128), F32),
             pltpu.VMEM((PEERS, 128), F32),
             pltpu.VMEM((CHUNK, CHUNK + 128), BF16),
@@ -504,8 +522,7 @@
             pltpu.VMEM((ROWS, SUBSETS), F32),
             pltpu.VMEM((24, SUBSETS), F32),
             pltpu.VMEM((8, SUBSETS), F32),
-            pltpu.VMEM((48, SUBSETS), F32),
-            pltpu.VMEM((128, SUBSETS), F32),
+            pltpu.VMEM((48, 128), F32),
             pltpu.VMEM((GRP, 1, 128), F32),
             pltpu.VMEM((SLAB, 1, 128), F32),
             pltpu.VMEM((GRP * 16, 128), F32),

time: 88.9 us -> 87.8 us (0.988)
  Pallas kernels: 85.9 us -> 84.8 us
    pallas_call x1, Pallas kernels: 85.9 us -> 84.8 us  [body(): pl.pallas_call(kernel, out_shape=(jax.ShapeDtypeStruct((8, PEERS * CAP),...]
where the time goes in v4:
time: 87.8 us; the launch traced here: 87.6 us
  Pallas kernels  84.8 us (97%)
  local copies, waits for them, and re-layouts  2.19 us (2%)
    pallas_call x1, Pallas kernels, body(): pl.pallas_call(kernel, out_shape=(jax.ShapeDtypeStruct((8, PEERS * CAP),...  84.8 us
    unnamed x4, local copies, waits for them, and re-layouts  2.19 us

profile of v4, /device:TPU:1, one launch (start us, length us, event | category | flops | bytes accessed | tf_op | source)
XLA Modules:
  0.0 87.6 jit_solution(18031909963644819846)
XLA Ops:
  0.6 84.8 %shard_map.86 = (f32[8,8192]{1,0:T(8,128)}, f32[1,8]{1,0:T(1,128)}) custom-call(s32[4,64]{1,0:T(4,128)} %bitcast.6, s32[64]{0:T(128)} %live_ref.1, bf16[27,2048]{1,0:T(8,128)(2,1)} %fields_ref.1, bf16[3,8,4,4096]{3,2,1,0:T(4,128)(2,1)} %spline_hbm.1, f32[3,4096]{1,0:T(4,128)} %meas_ref.1, f32[1,4096]{1,0:T(1,128)} %bitcast.4, s32[1,4096]{1,0:T(1,128)} %bitcast.5), custom_call_target="tpu_custom_call" | custom-call | tf_op jit(solution)/shard_map/pallas_call | solution.py:501
  85.4 0.0 copy-start
  85.5 1.7 %copy.11 = f32[8,8192]{1,0:T(8,128)} copy(f32[8,8192]{1,0:T(8,128)} %get-tuple-element.8) | data formatting | bytes 524288
  87.1 0.0 copy-done
  87.1 0.5 copy.12
Async XLA Ops:
  85.4 1.7 %copy-start = (f32[1,8]{1,0:T(1,128)S(1)}, f32[1,8]{1,0:T(1,128)}, u32[]{:S(2)}) copy-start(f32[1,8]{1,0:T(1,128)} %get-tuple-element.5) | copy-start | bytes 100

commit v5 on v4

--- a/solution.py
+++ b/solution.py
@@ -30,7 +30,8 @@
 CHUNK = 256
 CHUNKS = 16
 PEERS = 512
-HIGH = 64
+HIGH = 32
+LOW = 256
 
 
 def iota(shape, axis):
@@ -146,9 +147,9 @@
             onehot * (counted[:, :CHUNK] + jnp.concatenate([before, before], axis=1)), axis=0, keepdims=True
         )
         carry[...] = before + counted[:, CHUNK:]
-        low = ((owner >> 4) & 7) * CAP + rank.astype(jnp.int32)
-        high = (owner & 15) * 4 + (owner >> 7)
-        column = jnp.where(iota((128, CHUNK), 0) == low, 1.0, 0.0).T.astype(BF16)
+        low = (owner >> 8) * 128 + ((owner >> 4) & 7) * CAP + rank.astype(jnp.int32)
+        high = (owner & 15) * 2 + ((owner >> 7) & 1)
+        column = jnp.where(iota((LOW, CHUNK), 0) == low, 1.0, 0.0).T.astype(BF16)
         scatter_b[lanes, :] = column
         mask = jnp.where(iota((HIGH, CHUNK), 0) == high, 1.0, 0.0).astype(BF16)
         scatter_m[:, lanes] = mask
@@ -164,15 +165,14 @@
 
     both = (0, 1)
 
-    def send_step(p, step, position):
-        for direction in both:
-            @pl.when((step < STEPS - 1) | (p % 2 == direction))
-            def _():
-                hop(direction, p, position, 1 + (step % 3) // 2).start()
-
-            @pl.when(step % 3 == 2)
-            def _():
-                hop(direction, p, position, 1).start()
+    def send_step(direction, p, step, position):
+        @pl.when((step < STEPS - 1) | (p % 2 == direction))
+        def _():
+            hop(direction, p, position, 1 + (step % 3) // 2).start()
+
+        @pl.when(step % 3 == 2)
+        def _():
+            hop(direction, p, position, 1).start()
 
     for p in range(PIECES):
         for direction in both:
@@ -212,7 +212,7 @@
             for p in pieces:
                 for direction in both:
                     landed(direction, p, position)
-                send_step(p, step, position)
+                    send_step(direction, p, step, position)
             for p in pieces:
                 unpack_both(p, position)
 
@@ -229,7 +229,9 @@
     total = early_acc[0:4 * HIGH, :] + early_acc[4 * HIGH:, :]
     for c in range(4):
         for g in range(GRP):
-            early_out[16 * g + 4 * c:16 * g + 4 * c + 4, :] = total[HIGH * c + 4 * g:HIGH * c + 4 * g + 4, :]
+            for top in range(2):
+                start, source = 16 * g + 4 * c + 2 * top, HIGH * c + 2 * g
+                early_out[start:start + 2, :] = total[source:source + 2, 128 * top:128 * top + 128]
 
     def far_group(n):
         return GRP // 2 + (n // 2) * (2 * (n % 2) - 1)
@@ -301,6 +303,13 @@
             unpack_slots(p, [place_at(0, 8)])
 
     last_pieces((0, 1))
+
+    @pl.loop(1, GRP)
+    def _(j):
+        group_copy(early_out, early1, e1s, e1r, far_group(j), False).start()
+
+    mine = pl.ds(pl.multiple_of(16 * me_g, 16), 16)
+    early1[mine, :] = early_out[mine, :]
 
     @pl.loop(0, CHUNKS, unroll=2)
     def _(j):
@@ -373,13 +382,6 @@
     def _(j):
         reduce_copy(red2, r2s, r2r, far_slab(j) + SLAB - me_s, False, False).start()
 
-    @pl.loop(1, GRP)
-    def _(j):
-        group_copy(early_out, early1, e1s, e1r, far_group(j), False).start()
-
-    mine = pl.ds(pl.multiple_of(16 * me_g, 16), 16)
-    early1[mine, :] = early_out[mine, :]
-
     @pl.loop(1, SLAB)
     def _(j):
         reduce_copy(red2, r2s, r2r, j, True, False).wait_recv()
@@ -394,10 +396,8 @@
         pivot_row = system[i:i + 1, :] / system[i:i + 1, i:i + 1]
         system = jnp.where(sub == i, pivot_row, system - factor * pivot_row)
     update = system[:, 8:9]
-    flat = jnp.sum(jnp.where(lane == sub, update, 0.0), axis=0, keepdims=True)
-    upd_ref[...] = flat[:, :PARAMS]
-
-    placed = jnp.zeros((6 * HIGH, 128), F32)
+
+    placed = jnp.zeros((6 * HIGH, LOW), F32)
     for q in range(8):
         lanes = slice(512 * q, 512 * (q + 1))
         mask = scatter_m[:, lanes]
@@ -412,13 +412,18 @@
     placed = placed[:3 * HIGH] + placed[3 * HIGH:]
     for c in range(COMPS):
         for g in range(GRP):
-            late_out[g, c] = placed[HIGH * c + 4 * g:HIGH * c + 4 * g + 4, :]
+            for top in range(2):
+                source = HIGH * c + 2 * g
+                late_out[g, c, 2 * top:2 * top + 2, :] = placed[source:source + 2, 128 * top:128 * top + 128]
 
     @pl.loop(1, GRP)
     def _(j):
         group_copy(late_out, late1, d1s, d1r, far_group(j), False).start()
 
     late1[me_g] = late_out[me_g]
+
+    flat = jnp.sum(jnp.where(lane == sub, update, 0.0), axis=0, keepdims=True)
+    upd_ref[...] = flat[:, :PARAMS]
 
     @pl.loop(1, GRP)
     def _(j):
@@ -516,9 +521,9 @@
             pltpu.VMEM((PEERS, 128), F32),
             pltpu.VMEM((CHUNK, CHUNK + 128), BF16),
             pltpu.VMEM((BLOCKS * ROWS, PACKED), BF16),
-            pltpu.VMEM((SUBSETS, 128), BF16),
+            pltpu.VMEM((SUBSETS, LOW), BF16),
             pltpu.VMEM((HIGH, SUBSETS), BF16),
-            pltpu.VMEM((8 * HIGH, 128), F32),
+            pltpu.VMEM((8 * HIGH, LOW), F32),
             pltpu.VMEM((ROWS, SUBSETS), F32),
             pltpu.VMEM((24, SUBSETS), F32),
             pltpu.VMEM((8, SUBSETS), F32),

time: 87.8 us -> 88.6 us (level)
  Pallas kernels: 84.8 us -> 85.8 us
    pallas_call x1, Pallas kernels: 84.8 us -> 85.8 us  [body(): pl.pallas_call(kernel, out_shape=(jax.ShapeDtypeStruct((8, PEERS * CAP),...]
where the time goes in v5:
time: 88.6 us
  Pallas kernels  85.8 us (97%)
  local copies, waits for them, and re-layouts  2.19 us (2%)
    pallas_call x1, Pallas kernels, body(): pl.pallas_call(kernel, out_shape=(jax.ShapeDtypeStruct((8, PEERS * CAP),...  85.8 us
    unnamed x4, local copies, waits for them, and re-layouts  2.19 us

profile of v5, /device:TPU:1, one launch (start us, length us, event | category | flops | bytes accessed | tf_op | source)
XLA Modules:
  0.0 88.6 jit_solution(3471107970046486319)
XLA Ops:
  0.6 85.8 %shard_map.86 = (f32[8,8192]{1,0:T(8,128)}, f32[1,8]{1,0:T(1,128)}) custom-call(s32[4,64]{1,0:T(4,128)} %bitcast.6, s32[64]{0:T(128)} %live_ref.1, bf16[27,2048]{1,0:T(8,128)(2,1)} %fields_ref.1, bf16[3,8,4,4096]{3,2,1,0:T(4,128)(2,1)} %spline_hbm.1, f32[3,4096]{1,0:T(4,128)} %meas_ref.1, f32[1,4096]{1,0:T(1,128)} %bitcast.4, s32[1,4096]{1,0:T(1,128)} %bitcast.5), custom_call_target="tpu_custom_call" | custom-call | tf_op jit(solution)/shard_map/pallas_call | solution.py:506
  86.4 0.0 copy-start
  86.4 1.7 %copy.11 = f32[8,8192]{1,0:T(8,128)} copy(f32[8,8192]{1,0:T(8,128)} %get-tuple-element.8) | data formatting | bytes 524288
  88.1 0.0 copy-done
  88.1 0.5 copy.12
Async XLA Ops:
  86.4 1.7 %copy-start = (f32[1,8]{1,0:T(1,128)S(1)}, f32[1,8]{1,0:T(1,128)}, u32[]{:S(2)}) copy-start(f32[1,8]{1,0:T(1,128)} %get-tuple-element.5) | copy-start | bytes 100
